TPU v7x, 32 devices: a whole 2x2x4 slice. The times are simulated.
32 devices in a mesh: dp: 16 (over z, y, x), head: 2 (over core).
Axes of the slice: x: 2, y: 2, z: 4, core: 2. Of those that a mesh axis runs over, the one named last changes fastest.
Arguments:
- ids: int32 [16, 512], P('dp'), may hold values from 0 to 32127, as said below
- segments: int32 [16, 412], P('dp'), may hold values from 0 to 5, never falling along the last dimension, each value on 1 to 407 neighbouring positions
- valid_rows: int32 [16], P('dp'), may hold values from 1 to 412, as said below
- prompt: float32 [100, 768], replicated, may hold values from -6 to 6
- table: bfloat16 [32128, 768], P('dp'), may hold values from -6 to 6
- attn_gain: float32 [768], replicated, may hold values from 0.1 to 1.9
- w_qkv: bfloat16 [768, 3, 768], P(None, None, 'head'), may hold values from -0.21875 to 0.21875
- rel_bias: bfloat16 [32, 12], P(None, 'head'), may hold values from -4 to 4
- w_out: bfloat16 [768, 768], P('head'), may hold values from -1.75 to 1.75
- ff_gain: float32 [768], replicated, may hold values from 0.1 to 1.9
- w_in: bfloat16 [768, 3072], P(None, 'head'), may hold values from -0.21875 to 0.21875
- w_down: bfloat16 [3072, 768], P('head'), may hold values from -0.109375 to 0.109375
- cotangent: bfloat16 [8192, 768], P(('dp', 'head')), may hold values from -6 to 6
- first_moment: float32 [100, 768], replicated, may hold values from -3 to 3
- second_moment: float32 [100, 768], replicated, may hold values from 0.006666667 to 0.10666667
Outputs:
- layer_out: bfloat16 [8192, 768], P(('dp', 'head'))
- input_grad: float32 [8192, 768], P(('dp', 'head'))
- prompt_grad: float32 [100, 768], replicated
- grad_norm: float32 [], replicated
- prompt_new: float32 [100, 768], replicated
- first_out: float32 [100, 768], replicated
- second_out: float32 [100, 768], replicated
- prompt_low: bfloat16 [100, 768], replicated
Inputs may be any that keep to these rules, and one draw needn't show every extreme that they name: `ids`: positions t < 100 of each slot hold a permutation of 0 to 100 - 1 (prompt rows); every other position holds a vocabulary row, whose owner is id // 2008. Among the vocabulary positions of one device's 256 rows (positions b * 256 to (b + 1) * 256 - 1 of a slot) no owner is named more than 32 times, and in every share without prompt rows some owner is named exactly 32 times. The text rows of slot s at t - 100 >= valid_rows[s] are padding. The last slot has 412.
All inputs are finite; a program needn't handle non-finite values.
Results may differ from a plain program's by a relative error of at most 0.012.
The roundings to bfloat16 on the way count: a program that leaves them out, or rounds other values in their place, can miss the bound.
Values may be sent and summed in bfloat16 or wider, within the bound.
A program may use at most 192 MiB of HBM per device.

v0:
```python
import math

import jax
import jax.numpy as jnp
from jax import lax
from jax.sharding import PartitionSpec as P

STEP = 10


norm_epsilon = 1e-06
thresholds = (12, 16, 23, 32, 46, 64, 91)
masked_score = -1000000000.0
learn_rate = 0.5
first_decay = 0.5
second_decay = 0.75
weight_decay = 0.01
adam_epsilon = 1e-08
clip_share = 0.05
exact_mode = lax.Precision.HIGHEST


def rms_scale(rows, gain):
    return rows * lax.rsqrt(jnp.mean(rows * rows, axis=1, keepdims=True) + norm_epsilon) * gain


def rms_back(rows, gain, grad):
    return jax.vjp(lambda inner: rms_scale(inner, gain), rows)[1](grad)[0]


def bucket_of(relative):
    magnitude = jnp.abs(relative)
    larger = 8 + sum(((magnitude >= cutoff).astype(jnp.int32) for cutoff in thresholds))
    return jnp.where(magnitude < 8, magnitude, larger) + 16 * (relative > 0).astype(jnp.int32)


def rows_dot(left, right):
    return jnp.dot(left, right, preferred_element_type=jnp.float32)


def per_device(
    ids,
    segments,
    valid_rows,
    prompt,
    table,
    attn_gain,
    w_qkv,
    rel_bias,
    w_out,
    ff_gain,
    w_in,
    w_down,
    cotangent,
    first_moment,
    second_moment,
):
    heads_count = lax.axis_size("head")
    head_index = lax.axis_index("head")
    groups = lax.axis_size("dp")
    slot_len = ids.shape[1]
    share = slot_len // heads_count
    prompt_len = prompt.shape[0]
    width = prompt.shape[1]
    vocab_share = table.shape[0]
    capacity = max(2, 2 * slot_len // (heads_count * groups))
    spots = groups * capacity
    positions = head_index * share + jnp.arange(share, dtype=jnp.int32)
    row_ids = lax.dynamic_slice_in_dim(ids[0], head_index * share, share, 0)
    prompt_ids = ids[0, :prompt_len]
    in_prompt = positions < prompt_len
    owners = jnp.where(in_prompt, groups, row_ids // vocab_share)
    onehot = (owners[:, None] == jnp.arange(groups, dtype=jnp.int32)[None, :]).astype(jnp.int32)
    ranks = jnp.sum(jnp.cumsum(onehot, axis=0) * onehot, axis=1) - 1
    places = jnp.where(in_prompt, spots, owners * capacity + ranks)
    requests = (
        jnp.zeros((spots,), jnp.int32)
        .at[places]
        .set(row_ids - owners * vocab_share, mode="drop")
        .reshape(groups, capacity)
    )
    found = jnp.take(
        table, lax.all_to_all(requests, "dp", split_axis=0, concat_axis=0, tiled=True), axis=0
    )
    fetched = lax.all_to_all(found, "dp", split_axis=0, concat_axis=0, tiled=True).reshape(
        spots, width
    )
    text_rows = jnp.take(fetched, jnp.minimum(places, spots - 1), axis=0).astype(jnp.float32)
    prompt_rows = jnp.take(prompt, jnp.minimum(row_ids, prompt_len - 1), axis=0)
    x_start = jnp.where(in_prompt[:, None], prompt_rows, text_rows)
    cot_start = cotangent.astype(jnp.float32)
    seg_full = jnp.concatenate([jnp.full((prompt_len,), -1, jnp.int32), segments[0]])
    limit = prompt_len + valid_rows[0]
    key_pos = jnp.arange(slot_len, dtype=jnp.int32)
    key_ok = key_pos < limit
    row_first = head_index * share

    def spread(values, project):
        return project(lax.all_gather(values, "head", axis=0, tiled=True), jnp.int32(0))

    def collect(part_fn):
        return lax.psum_scatter(
            part_fn(jnp.int32(0), share * lax.axis_size("head")),
            "head",
            scatter_dimension=0,
            tiled=True,
        )

    heads_here = rel_bias.shape[1]
    inner_here = w_qkv.shape[2]
    head_size = inner_here // heads_here
    scale = head_size ** (-0.5)
    bias_table = rel_bias.T
    normed = rms_scale(x_start, attn_gain).astype(jnp.bfloat16)
    mixed = spread(
        normed,
        lambda piece, start: jnp.einsum(
            "rd,dcf->rcf", piece, w_qkv, preferred_element_type=jnp.float32
        ),
    ).astype(jnp.bfloat16)
    query_len = mixed.shape[0]
    queries = mixed[:, 0].reshape(query_len, heads_here, head_size)
    keys = mixed[:, 1].reshape(slot_len, heads_here, head_size)
    values = mixed[:, 2].reshape(slot_len, heads_here, head_size)
    block = min(512, query_len)
    starts = jnp.arange(query_len // block, dtype=jnp.int32) * block

    def scores_of(start):
        q_pos = start + jnp.arange(block, dtype=jnp.int32)
        bias = jnp.take(bias_table, bucket_of(key_pos[None, :] - q_pos[:, None]), axis=1)
        allowed = (key_pos < prompt_len)[None, :] | (
            seg_full[:, None] == seg_full[None, :]
        ) & key_ok[None, :]
        raw = (
            jnp.einsum("qhe,khe->hqk", queries, keys, preferred_element_type=jnp.float32) * scale
            + bias
        )
        return (jnp.where(allowed[None], raw, masked_score), queries)

    def forward_block(start):
        scores, q_block = scores_of(start)
        top = jnp.max(scores, axis=-1, keepdims=True)
        expo = jnp.exp(scores - top)
        total = jnp.sum(expo, axis=-1, keepdims=True)
        probs = (expo / total).astype(jnp.bfloat16)
        result = jnp.einsum("hqk,khe->qhe", probs, values, preferred_element_type=jnp.float32)
        return (
            result.reshape(block, inner_here).astype(jnp.bfloat16),
            (top + jnp.log(total))[..., 0],
        )

    out_blocks, lse_blocks = lax.map(forward_block, starts)
    attended = out_blocks.reshape(query_len, inner_here)
    middle = x_start + collect(lambda start, count: rows_dot(attended, w_out))
    normed_ff = rms_scale(middle, ff_gain).astype(jnp.bfloat16)
    hidden = spread(
        normed_ff, lambda piece, start: jnp.dot(piece, w_in, preferred_element_type=jnp.float32)
    )
    active = jax.nn.gelu(hidden).astype(jnp.bfloat16)
    final = middle + collect(lambda start, count: rows_dot(active, w_down))
    live = row_first + jnp.arange(x_start.shape[0], dtype=jnp.int32) < limit
    grad_out = cot_start * live[:, None].astype(jnp.float32)
    d_active = spread(
        grad_out.astype(jnp.bfloat16),
        lambda piece, start: jnp.einsum(
            "rd,fd->rf", piece, w_down, preferred_element_type=jnp.float32
        ),
    )
    d_hidden = jax.vjp(jax.nn.gelu, hidden)[1](d_active)[0].astype(jnp.bfloat16)
    d_normed_ff = collect(
        lambda start, count: jnp.einsum(
            "rf,df->rd", d_hidden, w_in, preferred_element_type=jnp.float32
        )
    )
    d_middle = grad_out + rms_back(middle, ff_gain, d_normed_ff)
    d_attended = spread(
        d_middle.astype(jnp.bfloat16),
        lambda piece, start: jnp.einsum(
            "rd,fd->rf", piece, w_out, preferred_element_type=jnp.float32
        ),
    ).astype(jnp.bfloat16)
    d_heads = d_attended.reshape(query_len, heads_here, head_size)

    def back_block(carry, inputs):
        d_keys, d_values = carry
        start, lse = inputs
        scores, q_block = scores_of(start)
        probs = jnp.exp(scores - lse[..., None])
        d_values = d_values + jnp.einsum(
            "hqk,qhe->khe", probs.astype(jnp.bfloat16), d_heads, preferred_element_type=jnp.float32
        )
        d_probs = jnp.einsum("qhe,khe->hqk", d_heads, values, preferred_element_type=jnp.float32)
        d_scores = (probs * (d_probs - jnp.sum(probs * d_probs, axis=-1, keepdims=True))).astype(
            jnp.bfloat16
        )
        d_query = (
            jnp.einsum("hqk,khe->qhe", d_scores, keys, preferred_element_type=jnp.float32) * scale
        )
        d_keys = (
            d_keys
            + jnp.einsum("hqk,qhe->khe", d_scores, q_block, preferred_element_type=jnp.float32)
            * scale
        )
        return ((d_keys, d_values), d_query.astype(jnp.bfloat16))

    empty = jnp.zeros((slot_len, heads_here, head_size), jnp.float32)
    (d_keys, d_values), d_queries = lax.scan(back_block, (empty, empty), (starts, lse_blocks))
    d_mixed = jnp.stack(
        [
            d_queries.reshape(query_len, inner_here),
            d_keys.reshape(slot_len, inner_here).astype(jnp.bfloat16),
            d_values.reshape(slot_len, inner_here).astype(jnp.bfloat16),
        ],
        axis=1,
    )
    d_normed = collect(
        lambda start, count: jnp.einsum(
            "rcf,dcf->rd", d_mixed, w_qkv, preferred_element_type=jnp.float32
        )
    )
    d_start = d_middle + rms_back(x_start, attn_gain, d_normed)
    order_pick = (prompt_ids[:, None] == jnp.arange(prompt_len, dtype=jnp.int32)[None, :]).astype(
        jnp.float32
    )
    partial_value = jnp.einsum(
        "rcf,dcf->rd", d_mixed[:prompt_len], w_qkv, preferred_element_type=jnp.float32
    )
    x_prompt = jnp.take(prompt, prompt_ids, axis=0)
    residual_part = jnp.where(head_index == 0, d_middle[:prompt_len], 0.0)
    local_grad = jnp.einsum(
        "tr,td->rd",
        order_pick,
        residual_part + rms_back(x_prompt, attn_gain, partial_value),
        precision=exact_mode,
    )
    prompt_grad = lax.psum(local_grad, ("dp", "head"))
    grad_norm = jnp.sqrt(jnp.sum(prompt_grad * prompt_grad))
    clip_at = clip_share * math.sqrt(prompt_len * width * groups)
    clipped = prompt_grad * jnp.minimum(1.0, clip_at / (grad_norm + 1e-06))
    first_out = first_decay * first_moment + (1.0 - first_decay) * clipped
    second_out = second_decay * second_moment + (1.0 - second_decay) * clipped * clipped
    first_hat = first_out / (1.0 - first_decay**STEP)
    second_hat = second_out / (1.0 - second_decay**STEP)
    prompt_new = prompt - learn_rate * (
        first_hat / (jnp.sqrt(second_hat) + adam_epsilon) + weight_decay * prompt
    )
    return (
        final.astype(jnp.bfloat16),
        d_start,
        prompt_grad,
        grad_norm,
        prompt_new,
        first_out,
        second_out,
        prompt_new.astype(jnp.bfloat16),
    )


def solution(mesh):
    in_specs = (
        P("dp", None),
        P("dp", None),
        P("dp"),
        P(),
        P("dp", None),
        P(),
        P(None, None, "head"),
        P(None, "head"),
        P("head", None),
        P(),
        P(None, "head"),
        P("head", None),
        P(("dp", "head"), None),
        P(),
        P(),
    )
    out_specs = (P(("dp", "head"), None), P(("dp", "head"), None), P(), P(), P(), P(), P(), P())
    return jax.shard_map(
        per_device, mesh=mesh, in_specs=in_specs, out_specs=out_specs, check_vma=False
    )
```

profile of v0, /device:TPU:1, one launch (start us, length us, event | category | flops | bytes accessed | tf_op | source)
XLA Modules:
  0.0 1241.9 jit_solution(7758650221878829904)
XLA Ops:
  11.2 7.4 all-to-all-start
  20.3 4.3 all-to-all-done
  24.7 2.7 gather_fusion.1
  29.7 3.6 all-to-all-start.1
  33.6 908.1 %gather_fusion.4 = bf16[262144,6]{1,0:T(8,128)(2,1)} fusion(bf16[6,32]{0,1:T(8,128)(2,1)S(1)} %bitcast.106, s32[262144]{0:T(1024)S(1)} %broadcast_clamp_fusion), kind=kCustom, calls=%fused_computation.clone | custom fusion | bytes 7340032 | tf_op jit(solution)/shard_map/while/body/eval_jaxpr/jit(_take)/gather | solution.py:130
  941.7 59.8 %copy.50 = bf16[512,512,6]{0,1,2:T(8,128)(2,1)} copy(bf16[512,512,6]{2,1,0:T(8,128)(2,1)} %bitcast.21) | data formatting | bytes 6291456 | tf_op jit(solution)/shard_map/while/body/eval_jaxpr/jit(_take)/gather | solution.py:130
  1007.1 4.4 all_gather.12
  1021.6 2.5 all_gather.14
  1024.1 7.9 reduce-scatter.5.cloned.1.call-done
  1033.6 2.4 all_gather.13
  1036.0 3.1 fusion.100
  1039.1 8.0 fusion.14
  1047.2 5.7 fusion.13
  1053.8 3.7 reduce-scatter.9.cloned.1.call-done
  1058.9 11.2 reduce-scatter.7.cloned.1.call-done
  1070.1 2.5 fusion.92
  1072.6 2.6 all_gather.15
  1076.9 3.9 fusion.18
  1086.5 2.3 multiply_reduce_fusion.7
  1090.1 3.9 convolution_bitcast_fusion
  1094.0 122.6 %all-reduce.3.cloned.1.call-done = f32[100,768]{1,0:T(8,128)} async-done(((f32[100,768]{1,0:T(8,128)}), f32[100,768]{1,0:T(8,128)}) %all-reduce.3.cloned.1.call-update) | async-done | bytes 307216 | tf_op jit(solution)/shard_map/psum | solution.py:236
  1219.0 2.6 fusion.90
  1221.6 7.7 reduce-scatter.11.cloned.1.call-done
  1230.8 2.7 fusion.39
  (137 shorter events, 39.5 us)
Async XLA Ops:
  7.2 17.6 %copy-start = (bf16[2008,768]{1,0:T(8,128)(2,1)S(1)}, bf16[2008,768]{1,0:T(8,128)(2,1)}, u32[]{:S(2)}) copy-start(bf16[2008,768]{1,0:T(8,128)(2,1)} %param.21) | copy-start | bytes 9252868
  11.2 13.5 %all-to-all-start = ((s32[16,1,32]{2,1,0:T(1,128)}), s32[16,1,32]{2,1,0:T(1,128)S(1)}, u32[]{:S(2)}, u32[]{:S(2)}) async-start(s32[16,1,32]{2,1,0:T(1,128)} %all_to_all.13), calls=%async_computation | async-start | bytes 16384 | tf_op jit(solution)/shard_map/all_to_all | solution.py:83
  27.4 5.9 copy-start.6
  27.5 6.1 copy-start.20
  29.7 975.7 %all-to-all-start.1 = ((bf16[16,32,768]{2,1,0:T(8,128)(2,1)}), bf16[16,32,768]{2,1,0:T(8,128)(2,1)S(1)}, u32[]{:S(2)}, u32[]{:S(2)}) async-start(bf16[16,32,768]{2,1,0:T(8,128)(2,1)} %broadcast_select_fusion), calls=%async_computation.1 | async-start | bytes 1572864 | tf_op jit(solution)/shard_map/all_to_all | solution.py:85
  33.3 998.7 %reduce-scatter.5.cloned.1.call-start = ((), (), s32[]{:S(2)}) async-start(), calls=%async_computation.6 | async-start | bytes 2359296 | tf_op jit(solution)/shard_map/reduce_scatter | solution.py:102
  1004.2 2.7 copy-start.18
  1006.6 4.9 copy-start.9
  1006.9 25.1 %copy-start.4 = (f32[256,768]{1,0:T(8,128)}, f32[256,768]{1,0:T(8,128)S(1)}, u32[]{:S(2)}) copy-start(f32[256,768]{1,0:T(8,128)S(1)} %get-tuple-element.75) | copy-start | bytes 2359300
  1012.7 3.0 copy-start.11
  1012.7 3.0 copy-start.13
  1021.4 12.1 copy-start.19
  1021.4 36.1 %reduce-scatter.9.cloned.1.call-start = ((), (), s32[]{:S(2)}) async-start(), calls=%async_computation.8 | async-start | bytes 2359296 | tf_op jit(solution)/shard_map/reduce_scatter | solution.py:102
  1032.0 4.0 copy-start.23
  1036.0 3.1 copy-start.15
  1047.1 5.8 copy-start.22
  1047.1 22.9 %reduce-scatter.7.cloned.1.call-start = ((), (), s32[]{:S(2)}) async-start(), calls=%async_computation.7 | async-start | bytes 2359296 | tf_op jit(solution)/shard_map/reduce_scatter | solution.py:102
  1052.9 163.7 %all-reduce.3.cloned.1.call-start = ((), (), s32[]{:S(2)}) async-start(), calls=%async_computation.10 | async-start | bytes 638976 | tf_op jit(solution)/shard_map/psum | solution.py:236
  1070.1 10.7 slice-start
  1072.6 16.2 %copy-start.5 = (f32[256,768]{1,0:T(8,128)}, f32[256,768]{1,0:T(8,128)S(1)}, u32[]{:S(2)}) copy-start(f32[256,768]{1,0:T(8,128)S(1)} %get-tuple-element.71) | copy-start | bytes 2359300
  1075.2 5.6 slice-start.1
  1090.0 139.2 %reduce-scatter.11.cloned.1.call-start = ((), (), s32[]{:S(2)}) async-start(), calls=%async_computation.9 | async-start | bytes 2359296 | tf_op jit(solution)/shard_map/reduce_scatter | solution.py:102
  1219.0 15.2 %copy-start.1 = (bf16[2008,768]{1,0:T(8,128)(2,1)S(1)}, bf16[2008,768]{1,0:T(8,128)(2,1)}, u32[]{:S(2)}) copy-start(bf16[2008,768]{1,0:T(8,128)(2,1)} %param.21) | copy-start | bytes 9252868
  1221.6 11.9 copy-start.8
  (9 other events, 15.2 us)
Sparse Core Ops, SparseCore 0:
  1021.5 10.4 reduce-scatter.4
  1047.3 10.2 reduce-scatter.8
  1059.8 10.2 reduce-scatter.6
  1090.2 126.4 all-reduce.2
  1218.7 10.5 reduce-scatter.10
where the time goes:
time: 1240 us
  local copies, waits for them, and re-layouts  982 us (79%)
  waiting for transfers between devices  158 us (13%)
  matrix products  39.3 us (3%)
  other arithmetic  23.4 us (2%)
  between operations  16.9 us (1%)
    gather x2, local copies, waits for them, and re-layouts, scores_of(): jnp.take(bias_table, bucket_of(key_pos[None, :] - q_pos[:, None]), axis=1)  968 us
    psum x1, waiting for transfers between devices, per_device(): prompt_grad = lax.psum(local_grad, ('dp', 'head'))  123 us
    reduce_scatter x4, waiting for transfers between devices, collect(): lax.psum_scatter(part_fn(jnp.int32(0), share * lax.axis_size('head')), 'h...  30.5 us
  transfers between devices with their start and end apart: 7, of which 6 were waited for; matrix products, arithmetic and copies ran while one was open for 80% of the time, Pallas kernels for 0%

commit v1 on v0

v1 whole, which is shorter than its diff:
```python
import functools
import math

import jax
import jax.numpy as jnp
from jax import lax
from jax.experimental import pallas as pl
from jax.experimental.pallas import tpu as pltpu
from jax.sharding import PartitionSpec as P

STEP = 10
norm_epsilon = 1e-06
thresholds = (12, 16, 23, 32, 46, 64, 91)
masked_score = -1000000000.0
learn_rate = 0.5
first_decay = 0.5
second_decay = 0.75
weight_decay = 0.01
adam_epsilon = 1e-08
clip_share = 0.05
exact_mode = lax.Precision.HIGHEST
MESH = pl.DeviceIdType.MESH
LANES = 128
SEND_ROWS = 8
NT = (((1,), (1,)), ((), ()))
NN = (((1,), (0,)), ((), ()))
TN = (((0,), (0,)), ((), ()))
f32 = jnp.float32
bf16 = jnp.bfloat16
GELU_C = math.sqrt(2.0 / math.pi)


def dot(left, right, dims=NN, precision=None):
    return lax.dot_general(left, right, dims, preferred_element_type=f32, precision=precision)


def rms_scale(rows, gain):
    return rows * lax.rsqrt(jnp.mean(rows * rows, axis=1, keepdims=True) + norm_epsilon) * gain


def rms_back(rows, gain, grad):
    r = lax.rsqrt(jnp.mean(rows * rows, axis=1, keepdims=True) + norm_epsilon)
    scaled = grad * gain
    return r * scaled - rows * (r * r * r * jnp.mean(rows * scaled, axis=1, keepdims=True))


def bucket_of(relative):
    magnitude = jnp.abs(relative)
    larger = 8 + sum(((magnitude >= cutoff).astype(jnp.int32) for cutoff in thresholds))
    return jnp.where(magnitude < 8, magnitude, larger) + 16 * (relative > 0).astype(jnp.int32)


def layer_kernel(
    x0_ref, cot_ref, mask_k_ref, mask_q_ref, bias_ref, order_ref, live_ref, ag_ref, fg_ref,
    wqkv_hbm, wout_hbm, win_hbm, wdown_hbm,
    out_ref, grad_ref, local_ref,
    wqkv, wout, win, wdown, k_all, v_all, kt, vt, qs, bias, probs, att_t, acc_out, acc_dn,
    dk_own, dv_own, dk_send, dv_send, dk_recv, dv_recv, dxb,
    wsem, kv_send, kv_recv, dkv_send, dkv_recv,
):
    dp = lax.axis_index("dp")
    head = lax.axis_index("head")
    other = (dp, 1 - head)
    share, width = x0_ref.shape
    slot = 2 * share
    pairs = width // LANES
    ff = win.shape[1]
    ff_block = 768
    mine = pl.ds(pl.multiple_of(head * share, share), share)
    theirs = pl.ds(pl.multiple_of((1 - head) * share, share), share)

    weight_copies = [
        pltpu.make_async_copy(src, dst, wsem.at[i])
        for i, (src, dst) in enumerate(
            ((wqkv_hbm, wqkv), (wout_hbm, wout), (win_hbm, win), (wdown_hbm, wdown))
        )
    ]
    for copy in weight_copies:
        copy.start()

    barrier = pltpu.get_barrier_semaphore()
    pl.semaphore_signal(barrier, inc=1, device_id=other, device_id_type=MESH)

    for h in range(2 * pairs):
        for d in range(5):
            base = jnp.broadcast_to(bias_ref[h, d : d + 1, :], (LANES, 2 * LANES))
            turned = pltpu.roll(base, 0, 1, stride=1, stride_axis=0)
            bias[h, d] = turned[:, :LANES]

    n1 = rms_scale(x0_ref[...], ag_ref[...]).astype(bf16)
    weight_copies[0].wait()
    k_all[mine, :] = dot(n1, wqkv[1]).astype(bf16)
    pl.semaphore_wait(barrier, 1)
    k_copy = pltpu.make_async_remote_copy(
        k_all.at[mine, :], k_all.at[mine, :], kv_send.at[0], kv_recv.at[0],
        device_id=other, device_id_type=MESH,
    )
    k_copy.start()
    v_all[mine, :] = dot(n1, wqkv[2]).astype(bf16)
    v_copy = pltpu.make_async_remote_copy(
        v_all.at[mine, :], v_all.at[mine, :], kv_send.at[1], kv_recv.at[1],
        device_id=other, device_id_type=MESH,
    )
    v_copy.start()
    q = dot(n1, wqkv[0]).astype(bf16) * jnp.asarray(0.125, bf16)
    lane = lax.broadcasted_iota(jnp.int32, (share, LANES), 1)
    for p in range(pairs):
        part = q[:, p * LANES : (p + 1) * LANES]
        qs[p, :share, :] = jnp.where(lane < LANES // 2, part, jnp.zeros_like(part))
        qs[p, share:, :] = jnp.where(lane >= LANES // 2, part, jnp.zeros_like(part))
    kt[head] = k_all[mine, :].T
    vt[head] = v_all[mine, :].T
    k_copy.wait()
    kt[1 - head] = k_all[theirs, :].T
    v_copy.wait()
    vt[1 - head] = v_all[theirs, :].T

    def forward(p, carry):
        cols = pl.ds(pl.multiple_of(p * LANES, LANES), LANES)
        left = jnp.concatenate([k_all[:, cols], mask_k_ref[...]], axis=1)
        mask_q = mask_q_ref[...]
        right = jnp.concatenate([qs[p], jnp.concatenate([mask_q, mask_q], axis=0)], axis=1)
        raw = dot(left, right, NT)
        rows = []
        for kb in range(slot // LANES):
            blocks = []
            for a in range(2):
                for qb in range(share // LANES):
                    apart = kb - (head * (share // LANES) + qb)
                    place = jnp.clip(apart, -2, 2) + 2
                    lo = a * share + qb * LANES
                    blocks.append(
                        raw[kb * LANES : (kb + 1) * LANES, lo : lo + LANES] + bias[2 * p + a, place]
                    )
            rows.append(jnp.concatenate(blocks, axis=1))
        scores = jnp.concatenate(rows, axis=0)
        expo = jnp.exp(scores - jnp.max(scores, axis=0, keepdims=True))
        prob = expo * (1.0 / jnp.sum(expo, axis=0, keepdims=True))
        probs[p] = prob
        low = prob.astype(bf16)
        half = LANES // 2
        for a in range(2):
            side = low[:, a * share : (a + 1) * share]
            feat = pl.ds(pl.multiple_of(p * LANES + a * half, half), half)
            att_t[feat, :] = (
                dot(vt[0, feat, :], side[:share]) + dot(vt[1, feat, :], side[share:])
            ).astype(bf16)
        return carry

    lax.fori_loop(0, pairs, forward, 0)
    weight_copies[1].wait()
    attended = att_t[...].T
    x1 = x0_ref[...] + dot(attended, wout[...])
    n2 = rms_scale(x1, fg_ref[...]).astype(bf16)
    dy = cot_ref[...] * live_ref[:, :1].astype(bf16)
    weight_copies[2].wait()
    weight_copies[3].wait()
    acc_out[...] = x1
    acc_dn[...] = jnp.zeros_like(acc_dn)

    def feed(i, carry):
        at = pl.ds(pl.multiple_of(i * ff_block, ff_block), ff_block)
        u = dot(n2, win[:, at])
        d_active = dot(dy, wdown[at, :], NT)
        square = u * u
        t = jnp.tanh(GELU_C * (u + 0.044715 * (u * square)))
        active = (0.5 * u * (1.0 + t)).astype(bf16)
        slope = 0.5 * (1.0 + t) + 0.5 * u * (1.0 - t * t) * (
            GELU_C * (1.0 + 3 * 0.044715 * square)
        )
        d_hidden = (d_active * slope).astype(bf16)
        acc_out[...] += dot(active, wdown[at, :])
        acc_dn[...] += dot(d_hidden, win[:, at], NT)
        return carry

    lax.fori_loop(0, ff // ff_block, feed, 0)
    out_ref[...] = acc_out[...].astype(bf16)
    dx1 = dy.astype(f32) + rms_back(x1, fg_ref[...], acc_dn[...])
    grad_ref[...] = dx1
    d_att = dot(dx1.astype(bf16), wout[...], NT).astype(bf16)
    for p in range(pairs):
        part = d_att[:, p * LANES : (p + 1) * LANES]
        dxb[p, :share, :] = jnp.where(lane < LANES // 2, part, jnp.zeros_like(part))
        dxb[p, share:, :] = jnp.where(lane >= LANES // 2, part, jnp.zeros_like(part))

    def send_of(p):
        return [
            pltpu.make_async_remote_copy(
                src.at[p], dst.at[p], dkv_send.at[i, p], dkv_recv.at[i, p],
                device_id=other, device_id_type=MESH,
            )
            for i, (src, dst) in enumerate(((dk_send, dk_recv), (dv_send, dv_recv)))
        ]

    def backward(p, carry):
        cols = pl.ds(pl.multiple_of(p * LANES, LANES), LANES)
        d_out = dxb[p]
        d_prob = dot(v_all[:, cols], d_out, NT)
        prob = probs[p]
        delta = jnp.sum(prob * d_prob, axis=0, keepdims=True)
        d_score = (prob * (d_prob - delta)).astype(bf16)
        low = prob.astype(bf16)
        half = LANES // 2
        for a in range(2):
            side = d_score[:, a * share : (a + 1) * share]
            feat = pl.ds(pl.multiple_of(p * LANES + a * half, half), half)
            att_t[feat, :] = (
                (dot(kt[0, feat, :], side[:share]) + dot(kt[1, feat, :], side[share:])) * 0.125
            ).astype(bf16)
        d_v = dot(low, d_out)
        d_k = dot(d_score, qs[p])
        first = head == 0
        dv_own[p] = jnp.where(first, d_v[:share], d_v[share:])
        dk_own[p] = jnp.where(first, d_k[:share], d_k[share:])
        dv_send[p] = jnp.where(first, d_v[share:], d_v[:share])
        dk_send[p] = jnp.where(first, d_k[share:], d_k[:share])
        for copy in send_of(p):
            copy.start()
        return carry

    lax.fori_loop(0, pairs, backward, 0)
    acc_dn[...] = dot(att_t[...].T, wqkv[0], NT)
    for p in range(pairs):
        for copy in send_of(p):
            copy.wait()
    d_k = jnp.concatenate([(dk_own[p] + dk_recv[p]).astype(bf16) for p in range(pairs)], axis=1)
    d_v = jnp.concatenate([(dv_own[p] + dv_recv[p]).astype(bf16) for p in range(pairs)], axis=1)
    d_n1 = acc_dn[...] + dot(d_k, wqkv[1], NT) + dot(d_v, wqkv[2], NT)
    total = grad_ref[...] + rms_back(x0_ref[...], ag_ref[...], d_n1)
    grad_ref[...] = total

    @pl.when(head == 0)
    def _():
        local_ref[...] = dot(order_ref[...], total[:LANES], TN, exact_mode)

    @pl.when(head != 0)
    def _():
        local_ref[...] = jnp.zeros_like(local_ref)


def vmem(*shape, dtype=f32):
    return pltpu.VMEM(shape, dtype)


def run_layer(x0, cot, mask_k, mask_q, bias, order, live, ag, fg, wqkv, wout, win, wdown):
    share, width = x0.shape
    ff = win.shape[1]
    pairs = width // LANES
    in_vmem = pl.BlockSpec(memory_space=pltpu.VMEM)
    in_hbm = pl.BlockSpec(memory_space=pl.ANY)
    return pl.pallas_call(
        layer_kernel,
        out_shape=(
            jax.ShapeDtypeStruct((share, width), bf16),
            jax.ShapeDtypeStruct((share, width), f32),
            jax.ShapeDtypeStruct((LANES, width), f32),
        ),
        in_specs=[in_vmem] * 9 + [in_hbm] * 4,
        out_specs=[in_vmem] * 3,
        scratch_shapes=[
            vmem(3, width, width, dtype=bf16),
            vmem(width, width, dtype=bf16),
            vmem(width, ff, dtype=bf16),
            vmem(ff, width, dtype=bf16),
            vmem(2 * share, width, dtype=bf16),
            vmem(2 * share, width, dtype=bf16),
            vmem(2, width, share, dtype=bf16),
            vmem(2, width, share, dtype=bf16),
            vmem(pairs, 2 * share, LANES, dtype=bf16),
            vmem(2 * pairs, 5, LANES, LANES),
            vmem(pairs, 2 * share, 2 * share),
            vmem(width, share, dtype=bf16),
            vmem(share, width),
            vmem(share, width),
        ]
        + [vmem(pairs, share, LANES)] * 6
        + [
            vmem(pairs, 2 * share, LANES, dtype=bf16),
            pltpu.SemaphoreType.DMA((4,)),
            pltpu.SemaphoreType.DMA((2,)),
            pltpu.SemaphoreType.DMA((2,)),
            pltpu.SemaphoreType.DMA((2, pairs)),
            pltpu.SemaphoreType.DMA((2, pairs)),
        ],
        compiler_params=pltpu.CompilerParams(
            collective_id=1, has_side_effects=True, vmem_limit_bytes=60 * 2**20
        ),
        name="layer",
    )(x0, cot, mask_k, mask_q, bias, order, live, ag, fg, wqkv, wout, win, wdown)


def update_kernel(
    inner, outer, clip_at,
    local_ref, prompt_ref, first_ref, second_ref,
    grad_ref, norm_ref, new_ref, first_out_ref, second_out_ref, low_ref,
    parts, group, total, send1, recv1, send2, recv2, send3, recv3, send4, recv4,
):
    dp = lax.axis_index("dp")
    head = lax.axis_index("head")
    rows = prompt_ref.shape[0]
    chunk = total.shape[0] // inner
    chunks = -(-rows // chunk)
    my_in = lax.rem(dp, inner)
    my_out = dp // inner
    barrier = pltpu.get_barrier_semaphore()

    def in_peer(k):
        return my_out * inner + lax.rem(my_in + k, inner)

    def out_peer(k):
        return lax.rem(my_out + k, outer) * inner + my_in

    def greet(device):
        pl.semaphore_signal(barrier, inc=1, device_id=device, device_id_type=MESH)

    greet((dp, 1 - head))

    def piece(index):
        return pl.ds(pl.multiple_of(index * chunk, chunk), chunk)

    def forward_of(index):
        return pltpu.make_async_remote_copy(
            total.at[piece(index), :], total.at[piece(index), :], send4.at[index], recv4.at[index],
            device_id=(dp, 1), device_id_type=MESH,
        )

    @pl.when(head == 0)
    def _():
        for k in range(1, inner):
            greet((in_peer(k), head))
        for k in range(1, outer):
            greet((out_peer(k), head))
        pl.semaphore_wait(barrier, inner + outer - 1)

        def scatter_to(k):
            target = lax.rem(my_in + k, inner)
            return target, pltpu.make_async_remote_copy(
                local_ref.at[piece(target), :], parts.at[my_in], send1.at[k], recv1.at[my_in],
                device_id=(in_peer(k), head), device_id_type=MESH,
            )

        def scatter_from(k):
            source = lax.rem(my_in + k, inner)
            return source, pltpu.make_async_remote_copy(
                local_ref.at[piece(source), :], parts.at[source], send1.at[k], recv1.at[source],
                device_id=(in_peer(k), head), device_id_type=MESH,
            )

        def gather_to(k):
            return pltpu.make_async_remote_copy(
                total.at[piece(my_in), :], total.at[piece(my_in), :], send2.at[k], recv2.at[my_in],
                device_id=(in_peer(k), head), device_id_type=MESH,
            )

        def gather_from(k):
            source = lax.rem(my_in + k, inner)
            return source, pltpu.make_async_remote_copy(
                total.at[piece(source), :], total.at[piece(source), :], send2.at[k],
                recv2.at[source], device_id=(in_peer(k), head), device_id_type=MESH,
            )

        def across(k):
            return pltpu.make_async_remote_copy(
                group.at[my_out], group.at[my_out], send3.at[k], recv3.at[my_out],
                device_id=(out_peer(k), head), device_id_type=MESH,
            )

        def across_from(k):
            source = lax.rem(my_out + k, outer)
            return pltpu.make_async_remote_copy(
                group.at[source], group.at[source], send3.at[k], recv3.at[source],
                device_id=(out_peer(k), head), device_id_type=MESH,
            )

        for k in range(1, inner):
            target, copy = scatter_to(k)

            @pl.when(target < chunks)
            def _():
                copy.start()

        @pl.when(my_in < chunks)
        def _():
            parts[my_in] = local_ref[piece(my_in), :]
            for k in range(1, inner):
                scatter_from(k)[1].wait_recv()
            summed = parts[0]
            for source in range(1, inner):
                summed = summed + parts[source]
            if outer > 1:
                group[my_out] = summed
                for k in range(1, outer):
                    across(k).start()
                for k in range(1, outer):
                    across_from(k).wait_recv()
                summed = group[0]
                for source in range(1, outer):
                    summed = summed + group[source]
                for k in range(1, outer):
                    across(k).wait_send()
            total[piece(my_in), :] = summed
            for k in range(1, inner):
                gather_to(k).start()
            forward_of(my_in).start()

        for k in range(1, inner):
            source, copy = gather_from(k)

            @pl.when(source < chunks)
            def _():
                copy.wait_recv()
                forward_of(source).start()

        for k in range(1, inner):
            target, copy = scatter_to(k)

            @pl.when(target < chunks)
            def _():
                copy.wait_send()

        @pl.when(my_in < chunks)
        def _():
            for k in range(1, inner):
                gather_to(k).wait_send()

    @pl.when(head == 1)
    def _():
        pl.semaphore_wait(barrier, 1)
        for index in range(chunks):
            forward_of(index).wait_recv()

    summed = total[:rows, :]
    grad_ref[...] = summed
    norm = jnp.sqrt(jnp.sum(summed * summed, keepdims=True))
    norm_ref[...] = norm
    clipped = summed * jnp.minimum(1.0, clip_at / (norm + 1e-06))
    first_out = first_decay * first_ref[...] + (1.0 - first_decay) * clipped
    second_out = second_decay * second_ref[...] + (1.0 - second_decay) * clipped * clipped
    first_hat = first_out / (1.0 - first_decay**STEP)
    second_hat = second_out / (1.0 - second_decay**STEP)
    prompt = prompt_ref[...]
    new = prompt - learn_rate * (
        first_hat / (jnp.sqrt(second_hat) + adam_epsilon) + weight_decay * prompt
    )
    first_out_ref[...] = first_out
    second_out_ref[...] = second_out
    new_ref[...] = new
    low_ref[...] = new.astype(bf16)

    @pl.when(head == 0)
    def _():
        for index in range(chunks):
            forward_of(index).wait_send()


def run_update(local, prompt, first, second, groups):
    inner = math.gcd(groups, 16)
    outer = groups // inner
    rows, width = prompt.shape
    padded = local.shape[0]
    chunk = padded // inner
    clip_at = clip_share * math.sqrt(rows * width * groups)
    shape = jax.ShapeDtypeStruct((rows, width), f32)
    spec = pl.BlockSpec(memory_space=pltpu.VMEM)
    return pl.pallas_call(
        functools.partial(update_kernel, inner, outer, clip_at),
        out_shape=(
            shape,
            jax.ShapeDtypeStruct((1, 1), f32),
            shape,
            shape,
            shape,
            jax.ShapeDtypeStruct((rows, width), bf16),
        ),
        in_specs=[spec] * 4,
        out_specs=[spec] * 6,
        scratch_shapes=[
            vmem(inner, chunk, width),
            vmem(outer, chunk, width),
            vmem(padded, width),
            pltpu.SemaphoreType.DMA((inner,)),
            pltpu.SemaphoreType.DMA((inner,)),
            pltpu.SemaphoreType.DMA((inner,)),
            pltpu.SemaphoreType.DMA((inner,)),
            pltpu.SemaphoreType.DMA((outer,)),
            pltpu.SemaphoreType.DMA((outer,)),
            pltpu.SemaphoreType.DMA((inner,)),
            pltpu.SemaphoreType.DMA((inner,)),
        ],
        compiler_params=pltpu.CompilerParams(
            collective_id=2, has_side_effects=True, vmem_limit_bytes=32 * 2**20
        ),
        name="update",
    )(local, prompt, first, second)


def per_device(
    ids,
    segments,
    valid_rows,
    prompt,
    table,
    attn_gain,
    w_qkv,
    rel_bias,
    w_out,
    ff_gain,
    w_in,
    w_down,
    cotangent,
    first_moment,
    second_moment,
):
    heads_count = lax.axis_size("head")
    head_index = lax.axis_index("head")
    groups = lax.axis_size("dp")
    slot_len = ids.shape[1]
    share = slot_len // heads_count
    prompt_len = prompt.shape[0]
    width = prompt.shape[1]
    vocab_share = table.shape[0]
    capacity = max(2, 2 * slot_len // (heads_count * groups))
    spots = groups * capacity
    positions = head_index * share + jnp.arange(share, dtype=jnp.int32)
    row_ids = lax.dynamic_slice_in_dim(ids[0], head_index * share, share, 0)
    prompt_ids = ids[0, :prompt_len]
    in_prompt = positions < prompt_len
    owners = jnp.where(in_prompt, groups, row_ids // vocab_share)
    onehot = (owners[:, None] == jnp.arange(groups, dtype=jnp.int32)[None, :]).astype(jnp.int32)
    ranks = jnp.sum(jnp.cumsum(onehot, axis=0) * onehot, axis=1) - 1
    places = jnp.where(in_prompt, spots, owners * capacity + ranks)
    requests = (
        jnp.zeros((spots,), jnp.int32)
        .at[places]
        .set(row_ids - owners * vocab_share, mode="drop")
        .reshape(groups, capacity)
    )
    found = jnp.take(
        table, lax.all_to_all(requests, "dp", split_axis=0, concat_axis=0, tiled=True), axis=0
    )
    fetched = lax.all_to_all(found, "dp", split_axis=0, concat_axis=0, tiled=True).reshape(
        spots, width
    )
    text_rows = jnp.take(fetched, jnp.minimum(places, spots - 1), axis=0).astype(jnp.float32)
    prompt_rows = jnp.take(prompt, jnp.minimum(row_ids, prompt_len - 1), axis=0)
    x_start = jnp.where(in_prompt[:, None], prompt_rows, text_rows)

    seg_full = jnp.concatenate([jnp.full((prompt_len,), -1, jnp.int32), segments[0]])
    limit = prompt_len + valid_rows[0]
    key_pos = jnp.arange(slot_len, dtype=jnp.int32)
    feature = jnp.arange(LANES, dtype=jnp.int32)[None, :] - 1
    allowed = (key_pos < prompt_len)[:, None] | (
        (seg_full[:, None] == feature) & (key_pos < limit)[:, None]
    )
    mask_k = jnp.where(allowed, 0.0, masked_score).astype(bf16)
    seg_here = lax.dynamic_slice_in_dim(seg_full, head_index * share, share, 0)
    mask_q = (seg_here[:, None] == feature).astype(bf16)
    live = jnp.broadcast_to((positions < limit)[:, None], (share, LANES)).astype(f32)
    full_bias = lax.all_gather(rel_bias.T, "head", axis=0, tiled=True).astype(f32)
    lag = (jnp.arange(2 * LANES, dtype=jnp.int32) + LANES) % (2 * LANES) - LANES
    apart = (jnp.arange(5, dtype=jnp.int32) - 2)[:, None] * LANES - lag[None, :]
    near = bucket_of(apart)
    near = jnp.where((jnp.arange(5) == 0)[:, None], 15, near)
    near = jnp.where((jnp.arange(5) == 4)[:, None], 31, near)
    pick = (near[:, :, None] == jnp.arange(rel_bias.shape[0])).astype(f32)
    bias_rows = jnp.einsum("djb,hb->hdj", pick, full_bias, precision=exact_mode)
    text = jnp.arange(LANES, dtype=jnp.int32)
    order = (
        (ids[0, :LANES][:, None] == text[None, :]) & (text < prompt_len)[:, None]
    ).astype(f32)

    full_qkv = lax.all_gather(jnp.transpose(w_qkv, (1, 0, 2)), "head", axis=2, tiled=True)
    full_out = lax.all_gather(w_out, "head", axis=0, tiled=True)
    full_in = lax.all_gather(w_in, "head", axis=1, tiled=True)
    full_down = lax.all_gather(w_down, "head", axis=0, tiled=True)

    final, d_start, local_grad = run_layer(
        x_start, cotangent, mask_k, mask_q, bias_rows, order, live,
        attn_gain.reshape(1, width), ff_gain.reshape(1, width),
        full_qkv, full_out, full_in, full_down,
    )
    prompt_grad, grad_norm, prompt_new, first_out, second_out, prompt_low = run_update(
        local_grad, prompt, first_moment, second_moment, groups
    )
    return (
        final,
        d_start,
        prompt_grad,
        grad_norm[0, 0],
        prompt_new,
        first_out,
        second_out,
        prompt_low,
    )


def solution(mesh):
    in_specs = (
        P("dp", None),
        P("dp", None),
        P("dp"),
        P(),
        P("dp", None),
        P(),
        P(None, None, "head"),
        P(None, "head"),
        P("head", None),
        P(),
        P(None, "head"),
        P("head", None),
        P(("dp", "head"), None),
        P(),
        P(),
    )
    out_specs = (P(("dp", "head"), None), P(("dp", "head"), None), P(), P(), P(), P(), P(), P())
    return jax.shard_map(
        per_device, mesh=mesh, in_specs=in_specs, out_specs=out_specs, check_vma=False
    )
```

time: 1240 us -> 146 us (0.12)
  local copies, waits for them, and re-layouts: 982 us -> 29 us
  waiting for transfers between devices: 158 us -> 27 us
  Pallas kernels: 0 us -> 49.6 us
  matrix products: 39.3 us -> 0.14 us
  other arithmetic: 23.4 us -> 8.02 us
    gather x3 -> x0, local copies, waits for them, and re-layouts: 969 us -> none  [the longest x2 968 us: scores_of(): jnp.take(bias_table, bucket_of(key_pos[None, :] - q_pos[:, None]), axis=1)]
    psum x1 -> x0, waiting for transfers between devices: 123 us -> none  [per_device(): prompt_grad = lax.psum(local_grad, ('dp', 'head'))]
    pallas_call x0 -> x2, Pallas kernels: none -> 49.6 us  [the longest x1 29.2 us: run_layer(): pl.pallas_call(layer_kernel, out_shape=(jax.ShapeDtypeStruct((share, widt...]
    dot_general x15 -> x1, matrix products: 39.3 us -> 0.14 us  [per_device(): bias_rows = jnp.einsum('djb,hb->hdj', pick, full_bias, precision=exact_mode)]
    reduce_scatter x4 -> x0, waiting for transfers between devices: 30.5 us -> none  [collect(): lax.psum_scatter(part_fn(jnp.int32(0), share * lax.axis_size('head')), 'h...]
    all_gather x0 -> x4, waiting for transfers between devices: none -> 13.5 us  [the longest x1 13.5 us: per_device(): full_down = lax.all_gather(w_down, 'head', axis=0, tiled=True)]
  transfers between devices with their start and end apart: 7 -> 6, of which waited for: 6 -> 3; matrix products, arithmetic and copies ran while one was open for 80% -> 14% of each run, Pallas kernels for 0% -> 0%
where the time goes in v1:
time: 146 us; the launch traced here: 145 us
  Pallas kernels  49.6 us (34%)
  local copies, waits for them, and re-layouts  29 us (20%)
  waiting for transfers between devices  27 us (18%)
  between operations  16.4 us (11%)
  starting transfers between devices  12.1 us (8%)
  other arithmetic  8.02 us (5%)
  blocking collectives  2.43 us (2%)
    pallas_call x1, Pallas kernels, run_layer(): pl.pallas_call(layer_kernel, out_shape=(jax.ShapeDtypeStruct((share, widt...  29.2 us
    pallas_call x1, Pallas kernels, run_update(): pl.pallas_call(functools.partial(update_kernel, inner, outer, clip_at), o...  20.4 us
    unnamed x38, local copies, waits for them, and re-layouts  15.2 us
    all_gather x1, waiting for transfers between devices, per_device(): full_down = lax.all_gather(w_down, 'head', axis=0, tiled=True)  13.5 us
    all_to_all x1, waiting for transfers between devices, per_device(): lax.all_to_all(found, 'dp', split_axis=0, concat_axis=0, tiled=True)  8.38 us
    all_to_all x1, starting transfers between devices, per_device(): lax.all_to_all(requests, 'dp', split_axis=0, concat_axis=0, tiled=True)  7.41 us
    all_to_all x1, starting transfers between devices, per_device(): lax.all_to_all(found, 'dp', split_axis=0, concat_axis=0, tiled=True)  4.49 us
    gather x1, local copies, waits for them, and re-layouts, per_device(): jnp.take(fetched, jnp.minimum(places, spots - 1), axis=0)  3.38 us
  transfers between devices with their start and end apart: 6, of which 3 were waited for; matrix products, arithmetic and copies ran while one was open for 14% of the time, Pallas kernels for 0%

profile of v1, /device:TPU:1, one launch (start us, length us, event | category | flops | bytes accessed | tf_op | source)
XLA Modules:
  0.0 144.6 jit_solution(3347093685686678360)
XLA Ops:
  11.0 1.4 scatter_custom_fusion
  13.1 7.4 %all-to-all-start = ((s32[16,1,32]{2,1,0:T(1,128)}), s32[16,1,32]{2,1,0:T(1,128)S(1)}, u32[]{:S(2)}, u32[]{:S(2)}) async-start(s32[16,1,32]{2,1,0:T(1,128)} %all_to_all.13), calls=%async_computation | async-start | bytes 16384 | tf_op jit(solution)/shard_map/all_to_all | solution.py:539
  21.2 2.4 %all-gather = bf16[2,6,32]{2,1,0:T(8,128)(2,1)S(1)} all-gather(bf16[1,6,32]{2,1,0:T(8,128)(2,1)S(1)} %bitcast.68), channel_id=1, replica_groups=mesh['dp'=16,'head'=2] {'head'}, dimensions={0}, use_global_device_ids=true | all-gather | bytes 1152 | tf_op jit(solution)/shard_map/all_gather | solution.py:559
  24.0 2.6 %all-to-all-done = s32[16,1,32]{2,1,0:T(1,128)S(1)} async-done(((s32[16,1,32]{2,1,0:T(1,128)}), s32[16,1,32]{2,1,0:T(1,128)S(1)}, u32[]{:S(2)}, u32[]{:S(2)}) %all-to-all-start) | async-done | bytes 2080 | tf_op jit(solution)/shard_map/all_to_all | solution.py:539
  26.7 2.7 %gather_fusion.1 = bf16[512,768]{1,0:T(8,128)(2,1)} fusion(bf16[2008,768]{1,0:T(8,128)(2,1)S(1)} %copy-done, s32[1024]{0:T(1024)S(1)} %pad_clamp_fusion.1), kind=kCustom, calls=%fused_computation.1 | custom fusion | bytes 1574912 | tf_op jit(solution)/shard_map/jit(_take)/gather | solution.py:538
  29.4 2.3 %broadcast_select_fusion = bf16[16,32,768]{2,1,0:T(8,128)(2,1)} fusion(bf16[16,32,768]{2,1,0:T(8,128)(2,1)} %bitcast.55, pred[16,32]{1,0:T(8,128)(4,1)S(1)} %compare_and_fusion), kind=kLoop, calls=%fused_computation.5 | loop fusion | flops 393216 | bytes 1573376 | tf_op jit(solution)/shard_map/jit(_take)/select_n | solution.py:538
  31.8 4.5 %all-to-all-start.1 = ((bf16[16,32,768]{2,1,0:T(8,128)(2,1)}), bf16[16,32,768]{2,1,0:T(8,128)(2,1)}, u32[]{:S(2)}, u32[]{:S(2)}) async-start(bf16[16,32,768]{2,1,0:T(8,128)(2,1)} %broadcast_select_fusion), calls=%async_computation.1 | async-start | bytes 1572864 | tf_op jit(solution)/shard_map/all_to_all | solution.py:541
  38.2 2.0 %gather_fusion = f32[256,768]{1,0:T(8,128)} fusion(f32[100,768]{1,0:T(8,128)S(1)} %copy-done.1, s32[1024]{0:T(1024)S(1)} %pad_clamp_fusion.2), kind=kCustom, calls=%fused_computation | custom fusion | bytes 1573888 | tf_op jit(solution)/shard_map/jit(_take)/gather | solution.py:545
  40.9 0.7 fusion.3.order_ref
  42.3 0.9 select_convert_fusion.mask_k_ref
  43.3 8.4 %all-to-all-done.1 = bf16[16,32,768]{2,1,0:T(8,128)(2,1)} async-done(((bf16[16,32,768]{2,1,0:T(8,128)(2,1)}), bf16[16,32,768]{2,1,0:T(8,128)(2,1)}, u32[]{:S(2)}, u32[]{:S(2)}) %all-to-all-start.1) | async-done | bytes 786464 | tf_op jit(solution)/shard_map/all_to_all | solution.py:541
  51.6 3.4 %gather_fusion.2 = bf16[256,768]{1,0:T(8,128)(2,1)} fusion(bf16[512,768]{1,0:T(8,128)(2,1)} %bitcast.12, s32[1024]{0:T(1024)S(1)} %pad_clamp_fusion), kind=kCustom, calls=%fused_computation.2 | custom fusion | bytes 787456 | tf_op jit(solution)/shard_map/jit(_take)/gather | solution.py:544
  55.0 2.3 %convert_select_fusion.x0_ref = f32[256,768]{1,0:T(8,128)} fusion(f32[256,768]{1,0:T(8,128)} %gather_fusion, bf16[256,768]{1,0:T(8,128)(2,1)} %gather_fusion.2, pred[256]{0:T(512)(128)(4,1)S(1)} %compare_and_fusion.2, pred[256]{0:T(512)(128)(4,1)S(1)} %compare_and_fusion.3, pred[256]{0:T(512)(128)(4,1)S(1)} %get-tuple-element.34), kind=kLoop, calls=%fused_computation.4 | loop fusion | flops 786432 | bytes 1966848 | tf_op jit(solution)/shard_map/jit(_where)/select_n | solution.py:546
  57.3 13.5 %all-gather.12.cloned.1.call-done.wdown_hbm = bf16[3072,768]{1,0:T(8,128)(2,1)} async-done(((bf16[1536,768]{1,0:T(8,128)(2,1)}), bf16[3072,768]{1,0:T(8,128)(2,1)}) %all-gather.12.cloned.1.call-update) | async-done | bytes 4718608 | tf_op jit(solution)/shard_map/all_gather | solution.py:575
  70.9 0.8 broadcast_in_dim.125.live_ref
  71.6 29.2 %layer.1 = (bf16[256,768]{1,0:T(8,128)(2,1)}, f32[256,768]{1,0:T(8,128)}, f32[128,768]{1,0:T(8,128)}) custom-call(f32[256,768]{1,0:T(8,128)} %convert_select_fusion.x0_ref, bf16[256,768]{1,0:T(8,128)(2,1)} %cot_ref.1, bf16[512,128]{1,0:T(8,128)(2,1)} %select_convert_fusion.mask_k_ref, bf16[256,128]{1,0:T(8,128)(2,1)} %compare_convert_fusion.mask_q_ref, ...), custom_call_target="tpu_custom_call" | custom-call | tf_op jit(solution)/shard_map/layer/pallas_call | solution.py:251
  100.8 1.0 copy-done.2
  101.8 1.0 copy-done.4
  102.8 20.4 %update.1 = (f32[100,768]{1,0:T(8,128)S(1)}, f32[1,1]{1,0:T(1,128)}, f32[100,768]{1,0:T(8,128)S(1)}, f32[100,768]{1,0:T(8,128)S(1)}, f32[100,768]{1,0:T(8,128)S(1)}, /*index=5*/bf16[100,768]{1,0:T(8,128)(2,1)S(1)}) custom-call(f32[128,768]{1,0:T(8,128)S(1)} %copy-done.2, f32[100,768]{1,0:T(8,128)S(1)} %copy-done.1, f32[100,768]{1,0:T(8,128)S(1)} %copy-done.3, ...), custom_call_target="tpu_custom_call" | custom-call | tf_op jit(solution)/shard_map/update/pallas_call | solution.py:465
  126.0 1.8 %copy.41 = bf16[256,768]{1,0:T(8,128)(2,1)} copy(bf16[256,768]{1,0:T(8,128)(2,1)} %get-tuple-element.47) | data formatting | bytes 786432
  127.8 2.1 %copy.42 = f32[256,768]{1,0:T(8,128)} copy(f32[256,768]{1,0:T(8,128)} %get-tuple-element.48) | data formatting | bytes 1572864
  131.2 1.7 %copy.45 = f32[100,768]{1,0:T(8,128)} copy(f32[100,768]{1,0:T(8,128)} %copy-done.8) | data formatting | bytes 614400
  133.0 1.7 %copy.46 = f32[100,768]{1,0:T(8,128)} copy(f32[100,768]{1,0:T(8,128)} %copy-done.7) | data formatting | bytes 614400
  135.4 1.6 %copy.48 = bf16[100,768]{1,0:T(8,128)(2,1)} copy(bf16[100,768]{1,0:T(8,128)(2,1)} %copy-done.9) | data formatting | bytes 307200
  (80 shorter events, 12.5 us)
Async XLA Ops:
  7.2 19.5 %copy-start = (bf16[2008,768]{1,0:T(8,128)(2,1)S(1)}, bf16[2008,768]{1,0:T(8,128)(2,1)}, u32[]{:S(2)}) copy-start(bf16[2008,768]{1,0:T(8,128)(2,1)} %param.19) | copy-start | bytes 9252868
  7.2 50.1 %all-gather.8.cloned.1.call-start = ((), (), s32[]{:S(2)}) async-start(), calls=%async_computation.3 | async-start | bytes 1769472 | tf_op jit(solution)/shard_map/all_gather | solution.py:573
  7.9 49.4 %all-gather.6.cloned.1.call-start = ((), (), s32[]{:S(2)}) async-start(), calls=%async_computation.2 | async-start | bytes 5308416 | tf_op jit(solution)/shard_map/all_gather | solution.py:572
  8.0 2.0 %copy-start.14 = (s32[1,512]{1,0:T(1,128)S(1)}, s32[1,512]{1,0:T(1,128)}, u32[]{:S(2)}) copy-start(s32[1,512]{1,0:T(1,128)} %param.15) | copy-start | bytes 6148
  8.0 13.2 %copy-start.13 = (bf16[32,6]{0,1:T(8,128)(2,1)S(1)}, bf16[32,6]{0,1:T(8,128)(2,1)}, u32[]{:S(2)}) copy-start(bf16[32,6]{0,1:T(8,128)(2,1)} %param.22) | copy-start | bytes 1156
  8.0 15.7 %copy-start.10 = (s32[1,412]{1,0:T(1,128)S(1)}, s32[1,412]{1,0:T(1,128)}, u32[]{:S(2)}) copy-start(s32[1,412]{1,0:T(1,128)} %param.16) | copy-start | bytes 4948
  8.7 48.7 %all-gather.10.cloned.1.call-start = ((), (), s32[]{:S(2)}) async-start(), calls=%async_computation.4 | async-start | bytes 7077888 | tf_op jit(solution)/shard_map/all_gather | solution.py:574
  9.4 61.5 %all-gather.12.cloned.1.call-start = ((), (), s32[]{:S(2)}) async-start(), calls=%async_computation.5 | async-start | bytes 7077888 | tf_op jit(solution)/shard_map/all_gather | solution.py:575
  13.1 13.5 %all-to-all-start = ((s32[16,1,32]{2,1,0:T(1,128)}), s32[16,1,32]{2,1,0:T(1,128)S(1)}, u32[]{:S(2)}, u32[]{:S(2)}) async-start(s32[16,1,32]{2,1,0:T(1,128)} %all_to_all.13), calls=%async_computation | async-start | bytes 16384 | tf_op jit(solution)/shard_map/all_to_all | solution.py:539
  29.4 6.9 %copy-start.11 = (f32[768]{0:T(1024)S(1)}, f32[768]{0:T(1024)}, u32[]{:S(2)}) copy-start(f32[768]{0:T(1024)} %param.20) | copy-start | bytes 9220
  29.4 7.5 %copy-start.12 = (f32[768]{0:T(1024)S(1)}, f32[768]{0:T(1024)}, u32[]{:S(2)}) copy-start(f32[768]{0:T(1024)} %param.24) | copy-start | bytes 9220
  29.4 8.8 %copy-start.1 = (f32[100,768]{1,0:T(8,128)S(1)}, f32[100,768]{1,0:T(8,128)}, u32[]{:S(2)}) copy-start(f32[100,768]{1,0:T(8,128)} %prompt_ref.1) | copy-start | bytes 921604
  31.8 19.9 %all-to-all-start.1 = ((bf16[16,32,768]{2,1,0:T(8,128)(2,1)}), bf16[16,32,768]{2,1,0:T(8,128)(2,1)}, u32[]{:S(2)}, u32[]{:S(2)}) async-start(bf16[16,32,768]{2,1,0:T(8,128)(2,1)} %broadcast_select_fusion), calls=%async_computation.1 | async-start | bytes 1572864 | tf_op jit(solution)/shard_map/all_to_all | solution.py:541
  71.6 29.2 %copy-start.3 = (f32[100,768]{1,0:T(8,128)S(1)}, f32[100,768]{1,0:T(8,128)}, u32[]{:S(2)}) copy-start(f32[100,768]{1,0:T(8,128)} %first_ref.1) | copy-start | bytes 921604
  100.8 1.0 copy-start.2
  101.8 1.0 copy-start.4
  123.2 0.7 copy-start.5
  123.9 0.7 copy-start.7
  124.6 0.7 copy-start.8
  125.4 0.7 copy-start.9
  126.0 8.7 %copy-start.6 = (f32[100,768]{1,0:T(8,128)S(1)}, f32[100,768]{1,0:T(8,128)}, u32[]{:S(2)}) copy-start(f32[100,768]{1,0:T(8,128)} %copy-done.5) | copy-start | bytes 921604
Sparse Core Ops, SparseCore 0:
  9.6 11.6 all-gather.7
  22.8 13.7 all-gather.5
  38.2 15.6 all-gather.9
  55.2 15.6 all-gather.11

commit v2 on v1

v2 whole, which is shorter than its diff:
```python
import functools
import math

import jax
import jax.numpy as jnp
from jax import lax
from jax.experimental import pallas as pl
from jax.experimental.pallas import tpu as pltpu
from jax.sharding import PartitionSpec as P

STEP = 10
norm_epsilon = 1e-06
thresholds = (12, 16, 23, 32, 46, 64, 91)
masked_score = -1000000000.0
learn_rate = 0.5
first_decay = 0.5
second_decay = 0.75
weight_decay = 0.01
adam_epsilon = 1e-08
clip_share = 0.05
exact_mode = lax.Precision.HIGHEST
MESH = pl.DeviceIdType.MESH
LANES = 128
NT = (((1,), (1,)), ((), ()))
NN = (((1,), (0,)), ((), ()))
TN = (((0,), (0,)), ((), ()))
f32 = jnp.float32
bf16 = jnp.bfloat16
GELU_C = math.sqrt(2.0 / math.pi)


def dot(left, right, dims=NN, precision=None):
    return lax.dot_general(left, right, dims, preferred_element_type=f32, precision=precision)


def rms_scale(rows, gain):
    return rows * lax.rsqrt(jnp.mean(rows * rows, axis=1, keepdims=True) + norm_epsilon) * gain


def rms_back(rows, gain, grad):
    r = lax.rsqrt(jnp.mean(rows * rows, axis=1, keepdims=True) + norm_epsilon)
    scaled = grad * gain
    return r * scaled - rows * (r * r * r * jnp.mean(rows * scaled, axis=1, keepdims=True))


def bucket_of(relative):
    magnitude = jnp.abs(relative)
    larger = 8 + sum(((magnitude >= cutoff).astype(jnp.int32) for cutoff in thresholds))
    return jnp.where(magnitude < 8, magnitude, larger) + 16 * (relative > 0).astype(jnp.int32)


def each(count, body):
    if count <= 16:
        for i in range(count):
            body(i)
    else:
        lax.fori_loop(0, count, lambda i, carry: (body(i), carry)[1], 0)


def layer_kernel(
    groups, inner, block, rows,
    ids_ref, seg_ref, valid_ref, prompt_ref, ag_ref, fg_ref, rel_ref, cot_ref,
    table_hbm, wqkv_hbm, wout_hbm, win_hbm, wdown_hbm,
    out_hbm, grad_hbm, total_hbm,
    table, wqkv, wout, win, wdown,
    req_out, req_in, found, fetched, rel_all, prompt_pad, seg_pad, mask_k, mask_q,
    x0, x0_prompt, d_act, out_buf, grad_buf,
    k_all, v_all, kt, vt, qs, bias, probs, att_t, acc_out, acc_dn,
    dk_own, dv_own, dk_send, dv_send, dk_recv, dv_recv, dxb,
    rs_send, parts, across_buf, total,
    load_sem, far_send, far_recv, req_send, req_recv, row_send, row_recv,
    kv_send, kv_recv, dkv_send, dkv_recv,
    send1, recv1, send2, recv2, send3, recv3, send4, recv4, out_sem,
):
    dp = lax.axis_index("dp")
    head = lax.axis_index("head")
    other = (dp, 1 - head)
    share, width = x0.shape
    slot = 2 * share
    pairs = width // LANES
    half_width = width // 2
    ff = win.shape[1]
    half_ff = ff // 2
    ff_block = d_act.shape[2]
    vocab = table.shape[0]
    spots = groups * block
    outer = groups // inner
    my_in = lax.rem(dp, inner)
    my_out = dp // inner
    mine = pl.ds(pl.multiple_of(head * share, share), share)
    theirs = pl.ds(pl.multiple_of((1 - head) * share, share), share)

    def remote(src, dst, send, recv, device):
        return pltpu.make_async_remote_copy(
            src, dst, send, recv, device_id=device, device_id_type=MESH
        )

    my_cols = pl.ds(pl.multiple_of(head * half_width, half_width), half_width)
    my_ff = pl.ds(pl.multiple_of(head * half_ff, half_ff), half_ff)
    weight_pairs = (
        (wdown_hbm, wdown.at[my_ff, :]),
        (wqkv_hbm, wqkv.at[:, :, my_cols]),
        (wout_hbm, wout.at[my_cols, :]),
        (win_hbm, win.at[:, my_ff]),
    )
    table_copy = pltpu.make_async_copy(table_hbm, table, load_sem.at[4])
    table_copy.start()
    local_copies = [
        pltpu.make_async_copy(src, dst, load_sem.at[i]) for i, (src, dst) in enumerate(weight_pairs)
    ]
    for copy in local_copies:
        copy.start()
    far_copies = [
        remote(src, dst, far_send.at[i], far_recv.at[i], other)
        for i, (src, dst) in enumerate(weight_pairs)
    ]

    barrier = pltpu.get_barrier_semaphore()

    def greet(k):
        pl.semaphore_signal(
            barrier, inc=1, device_id=(lax.rem(dp + 1 + k, groups), head), device_id_type=MESH
        )

    pl.semaphore_signal(barrier, inc=1, device_id=other, device_id_type=MESH)
    each(groups - 1, greet)

    lane = lax.broadcasted_iota(jnp.int32, (share, LANES), 1)
    row = lax.broadcasted_iota(jnp.int32, (share, LANES), 0) + head * share
    lane_f = lane.astype(f32)
    row_ids = ids_ref[:, mine].astype(f32)
    ids_col = jnp.concatenate(
        [
            jnp.broadcast_to(row_ids[:, i * LANES : (i + 1) * LANES], (LANES, LANES)).T
            for i in range(share // LANES)
        ],
        axis=0,
    )
    is_text = row >= rows
    owner = jnp.where(is_text, jnp.floor((ids_col + 0.5) * (1.0 / vocab)), -1.0)
    hot = (owner == lane_f).astype(f32)
    tri_row = lax.broadcasted_iota(jnp.int32, (share, share), 0)
    tri_col = lax.broadcasted_iota(jnp.int32, (share, share), 1)
    earlier = (tri_row > tri_col).astype(f32).astype(bf16)
    rank = jnp.sum(dot(earlier, hot.astype(bf16)) * hot, axis=1, keepdims=True)
    place = jnp.where(is_text[:, :1], owner[:, :1] * block + rank, -1.0)
    ranked = (rank == lane_f).astype(f32)
    wanted = dot(hot * (ids_col - owner * vocab), ranked, TN, exact_mode)
    for o in range(groups):
        req_out[o] = wanted[o : o + 1, :]

    order = jnp.where(is_text[:LANES], 0.0, (ids_col[:LANES] == lane_f[:LANES]).astype(f32))

    rel_all[head] = jnp.zeros((8, LANES), f32)
    rel_all[head, : rel_ref.shape[0], : rel_ref.shape[1]] = rel_ref[...].astype(f32)

    seg_pad[:, : seg_ref.shape[1]] = seg_ref[...]
    lanes_slot = lax.broadcasted_iota(jnp.int32, (1, slot), 1)
    seg_row = jnp.where(lanes_slot < rows, -1, pltpu.roll(seg_pad[...], rows, 1)).astype(f32)
    limit = valid_ref[0] + rows
    square_lane = lax.broadcasted_iota(jnp.int32, (LANES, LANES), 1).astype(f32) - 1.0
    square_row = lax.broadcasted_iota(jnp.int32, (LANES, LANES), 0)
    for kb in range(slot // LANES):
        at = kb * LANES
        seg_col = jnp.broadcast_to(seg_row[:, at : at + LANES], (LANES, LANES)).T
        same = seg_col == square_lane
        key = square_row + at
        allowed = (key < rows) | (same & (key < limit))
        mask_k[at : at + LANES, :] = jnp.where(allowed, 0.0, masked_score).astype(bf16)

        @pl.when(head == at // share)
        def _():
            mask_q[at % share : at % share + LANES, :] = same.astype(f32).astype(bf16)

    live = row[:, :1] < limit
    dy = jnp.where(live, cot_ref[...].astype(f32), 0.0).astype(bf16)

    pl.semaphore_wait(barrier, groups)
    req_in[dp] = req_out[dp]

    def request_to(k):
        peer = lax.rem(dp + 1 + k, groups)
        return remote(
            req_out.at[peer], req_in.at[dp], req_send.at[peer], req_recv.at[dp], (peer, head)
        )

    def request_from(k):
        peer = lax.rem(dp + 1 + k, groups)
        return remote(
            req_out.at[peer], req_in.at[peer], req_send.at[peer], req_recv.at[peer], (peer, head)
        )

    each(groups - 1, lambda k: request_to(k).start())
    rel_copy = remote(
        rel_all.at[head], rel_all.at[head], far_send.at[4], far_recv.at[4], other
    )
    rel_copy.start()
    for copy in far_copies:
        copy.start()

    local_copies[0].wait()

    def activation_grad(index):
        at = pl.ds(pl.multiple_of(index * ff_block, ff_block), ff_block)
        d_act[index] = dot(dy, wdown[at, :], NT)

    half_blocks = half_ff // ff_block
    for i in range(half_blocks):
        activation_grad(head * half_blocks + i)

    table_copy.wait()
    each(groups - 1, lambda k: request_from(k).wait_recv())
    vocab_lane = lax.broadcasted_iota(jnp.int32, (block, vocab), 1).astype(f32)
    bunch = 8

    def row_to(peer):
        return remote(
            found.at[peer], fetched.at[dp], row_send.at[peer], row_recv.at[dp], (peer, head)
        )

    def row_from(peer):
        return remote(
            found.at[peer], fetched.at[peer], row_send.at[peer], row_recv.at[peer], (peer, head)
        )

    def serve(g):
        base = lax.rem(dp // bunch + 1 + g, groups // bunch) * bunch
        wants = jnp.concatenate(
            [req_in[base + j] for j in range(bunch)] + [jnp.zeros((LANES - bunch, LANES), f32)],
            axis=0,
        ).T
        picks = jnp.concatenate(
            [
                (wants[:block, j : j + 1] == vocab_lane).astype(f32).astype(bf16)
                for j in range(bunch)
            ],
            axis=0,
        )
        picked = dot(picks, table[...]).astype(bf16)
        for j in range(bunch):
            found[base + j] = picked[j * block : (j + 1) * block]

            @pl.when(base + j != dp)
            def _():
                row_to(base + j).start()

    each(groups // bunch, serve)
    fetched[dp] = found[dp]

    @pl.when(head == 0)
    def _():
        prompt_pad[...] = jnp.zeros_like(prompt_pad)
        prompt_pad[:rows, :] = prompt_ref[...]
        x0_prompt[...] = dot(order, prompt_pad[...], NN, exact_mode)

    rel_copy.wait()
    spread = lax.broadcasted_iota(jnp.int32, (1, 2 * LANES), 1)
    lag = jnp.where(spread >= LANES, spread - 2 * LANES, spread)
    bucket_row = lax.broadcasted_iota(jnp.int32, (LANES, 2 * LANES), 0)
    for d in range(5):
        if d == 0:
            near = jnp.full((1, 2 * LANES), 15, jnp.int32)
        elif d == 4:
            near = jnp.full((1, 2 * LANES), 31, jnp.int32)
        else:
            near = bucket_of((d - 2) * LANES - lag)
        pick = (bucket_row == near).astype(f32).astype(bf16)
        for side in range(2):
            lines = dot(rel_all[side].astype(bf16), pick)
            for h in range(pairs):
                line = jnp.broadcast_to(lines[h : h + 1, :], (LANES, 2 * LANES))
                if d not in (0, 4):
                    line = pltpu.roll(line, 0, 1, stride=1, stride_axis=0)
                bias[side * pairs + h, d] = line[:, :LANES]

    far_copies[0].wait()
    for i in range(half_blocks):
        activation_grad((1 - head) * half_blocks + i)
    for copy in local_copies[1:]:
        copy.wait()
    far_copies[1].wait()

    for peer in range(groups) if groups <= 16 else ():

        @pl.when(peer != dp)
        def _():
            row_from(peer).wait_recv()

    if groups > 16:
        each(groups - 1, lambda k: row_from(lax.rem(dp + 1 + k, groups)).wait_recv())
    spot_lane = lax.broadcasted_iota(jnp.int32, (share, spots), 1).astype(f32)
    take = (place == spot_lane).astype(f32).astype(bf16)
    x0[...] = dot(take, fetched[...].reshape(spots, width))

    @pl.when(head == 0)
    def _():
        x0[:LANES, :] = x0[:LANES, :] + x0_prompt[...]

    attn_gain = ag_ref[...].reshape(1, width)
    ff_gain = fg_ref[...].reshape(1, width)
    n1 = rms_scale(x0[...], attn_gain).astype(bf16)
    k_all[mine, :] = dot(n1, wqkv[1]).astype(bf16)
    k_copy = remote(
        k_all.at[mine, :], k_all.at[mine, :], kv_send.at[0], kv_recv.at[0], other
    )
    k_copy.start()
    v_all[mine, :] = dot(n1, wqkv[2]).astype(bf16)
    v_copy = remote(
        v_all.at[mine, :], v_all.at[mine, :], kv_send.at[1], kv_recv.at[1], other
    )
    v_copy.start()
    q = dot(n1, wqkv[0]).astype(bf16) * jnp.asarray(0.125, bf16)
    for p in range(pairs):
        part = q[:, p * LANES : (p + 1) * LANES]
        qs[p, :share, :] = jnp.where(lane < LANES // 2, part, jnp.zeros_like(part))
        qs[p, share:, :] = jnp.where(lane >= LANES // 2, part, jnp.zeros_like(part))
    kt[head] = k_all[mine, :].T
    vt[head] = v_all[mine, :].T
    k_copy.wait()
    kt[1 - head] = k_all[theirs, :].T
    v_copy.wait()
    vt[1 - head] = v_all[theirs, :].T

    def forward(p, carry):
        cols = pl.ds(pl.multiple_of(p * LANES, LANES), LANES)
        left = jnp.concatenate([k_all[:, cols], mask_k[...]], axis=1)
        right = jnp.concatenate(
            [qs[p], jnp.concatenate([mask_q[...], mask_q[...]], axis=0)], axis=1
        )
        raw = dot(left, right, NT)
        bands = []
        for kb in range(slot // LANES):
            blocks = []
            for a in range(2):
                for qb in range(share // LANES):
                    apart = kb - (head * (share // LANES) + qb)
                    spot = jnp.clip(apart, -2, 2) + 2
                    lo = a * share + qb * LANES
                    blocks.append(
                        raw[kb * LANES : (kb + 1) * LANES, lo : lo + LANES] + bias[2 * p + a, spot]
                    )
            bands.append(jnp.concatenate(blocks, axis=1))
        scores = jnp.concatenate(bands, axis=0)
        expo = jnp.exp(scores - jnp.max(scores, axis=0, keepdims=True))
        prob = expo * (1.0 / jnp.sum(expo, axis=0, keepdims=True))
        probs[p] = prob
        low = prob.astype(bf16)
        half = LANES // 2
        for a in range(2):
            side = low[:, a * share : (a + 1) * share]
            feat = pl.ds(pl.multiple_of(p * LANES + a * half, half), half)
            att_t[feat, :] = (
                dot(vt[0, feat, :], side[:share]) + dot(vt[1, feat, :], side[share:])
            ).astype(bf16)
        return carry

    lax.fori_loop(0, pairs, forward, 0)
    far_copies[2].wait()
    x1 = x0[...] + dot(att_t[...].T, wout[...])
    n2 = rms_scale(x1, ff_gain).astype(bf16)
    far_copies[3].wait()
    acc_out[...] = x1
    acc_dn[...] = jnp.zeros_like(acc_dn)

    def feed(i, carry):
        at = pl.ds(pl.multiple_of(i * ff_block, ff_block), ff_block)
        u = dot(n2, win[:, at])
        square = u * u
        t = jnp.tanh(GELU_C * (u + 0.044715 * (u * square)))
        active = (0.5 * u * (1.0 + t)).astype(bf16)
        slope = 0.5 * (1.0 + t) + 0.5 * u * (1.0 - t * t) * (
            GELU_C * (1.0 + 3 * 0.044715 * square)
        )
        d_hidden = (d_act[i] * slope).astype(bf16)
        acc_out[...] += dot(active, wdown[at, :])
        acc_dn[...] += dot(d_hidden, win[:, at], NT)
        return carry

    lax.fori_loop(0, ff // ff_block, feed, 0)
    out_buf[...] = acc_out[...].astype(bf16)
    out_copy = pltpu.make_async_copy(out_buf, out_hbm, out_sem.at[0])
    out_copy.start()
    dx1 = dy.astype(f32) + rms_back(x1, ff_gain, acc_dn[...])
    grad_buf[...] = dx1
    d_att = dot(dx1.astype(bf16), wout[...], NT).astype(bf16)
    for p in range(pairs):
        part = d_att[:, p * LANES : (p + 1) * LANES]
        dxb[p, :share, :] = jnp.where(lane < LANES // 2, part, jnp.zeros_like(part))
        dxb[p, share:, :] = jnp.where(lane >= LANES // 2, part, jnp.zeros_like(part))

    def send_of(p):
        return [
            remote(src.at[p], dst.at[p], dkv_send.at[i, p], dkv_recv.at[i, p], other)
            for i, (src, dst) in enumerate(((dk_send, dk_recv), (dv_send, dv_recv)))
        ]

    def backward(p, carry):
        cols = pl.ds(pl.multiple_of(p * LANES, LANES), LANES)
        d_out = dxb[p]
        d_prob = dot(v_all[:, cols], d_out, NT)
        prob = probs[p]
        delta = jnp.sum(prob * d_prob, axis=0, keepdims=True)
        d_score = (prob * (d_prob - delta)).astype(bf16)
        low = prob.astype(bf16)
        half = LANES // 2
        for a in range(2):
            side = d_score[:, a * share : (a + 1) * share]
            feat = pl.ds(pl.multiple_of(p * LANES + a * half, half), half)
            att_t[feat, :] = (
                (dot(kt[0, feat, :], side[:share]) + dot(kt[1, feat, :], side[share:])) * 0.125
            ).astype(bf16)
        d_v = dot(low, d_out)
        d_k = dot(d_score, qs[p])
        first = head == 0
        dv_own[p] = jnp.where(first, d_v[:share], d_v[share:])
        dk_own[p] = jnp.where(first, d_k[:share], d_k[share:])
        dv_send[p] = jnp.where(first, d_v[share:], d_v[:share])
        dk_send[p] = jnp.where(first, d_k[share:], d_k[:share])
        for copy in send_of(p):
            copy.start()
        return carry

    lax.fori_loop(0, pairs, backward, 0)
    acc_dn[...] = dot(att_t[...].T, wqkv[0], NT)
    for p in range(pairs):
        for copy in send_of(p):
            copy.wait()
    d_k = jnp.concatenate([(dk_own[p] + dk_recv[p]).astype(bf16) for p in range(pairs)], axis=1)
    d_v = jnp.concatenate([(dv_own[p] + dv_recv[p]).astype(bf16) for p in range(pairs)], axis=1)
    d_n1 = acc_dn[...] + dot(d_k, wqkv[1], NT) + dot(d_v, wqkv[2], NT)
    grad_buf[...] = grad_buf[...] + rms_back(x0[...], attn_gain, d_n1)
    grad_copy = pltpu.make_async_copy(grad_buf, grad_hbm, out_sem.at[1])
    grad_copy.start()

    chunks, chunk_rows, chunk_cols = total.shape

    def forward_of(index):
        return remote(
            total.at[index], total.at[index], send4.at[index], recv4.at[index], (dp, 1)
        )

    def in_peer(k):
        target = lax.rem(my_in + k, inner)
        return target, (my_out * inner + target, head)

    def out_peer(k):
        target = lax.rem(my_out + k, outer)
        return target, (target * inner + my_in, head)

    @pl.when(head == 0)
    def _():
        local = dot(order, grad_buf[:LANES, :], TN, exact_mode).astype(bf16)
        for c in range(chunks):
            top, left = (c // 2) * chunk_rows, (c % 2) * chunk_cols
            rs_send[c] = local[top : top + chunk_rows, left : left + chunk_cols]

        def scatter_to(k):
            target, device = in_peer(k)
            return target, remote(
                rs_send.at[jnp.minimum(target, chunks - 1)], parts.at[my_in], send1.at[k], recv1.at[my_in], device
            )

        def scatter_from(k):
            source, device = in_peer(k)
            return remote(
                rs_send.at[0], parts.at[source], send1.at[k], recv1.at[source], device
            )

        mine_in = jnp.minimum(my_in, chunks - 1)

        def gather_to(k):
            return remote(
                total.at[mine_in], total.at[mine_in], send2.at[k], recv2.at[mine_in], in_peer(k)[1]
            )

        def gather_from(k):
            source, device = in_peer(k)
            at = jnp.minimum(source, chunks - 1)
            return source, at, remote(
                total.at[at], total.at[at], send2.at[k], recv2.at[at], device
            )

        def across(k):
            return remote(
                across_buf.at[my_out], across_buf.at[my_out], send3.at[k], recv3.at[my_out],
                out_peer(k)[1],
            )

        def across_from(k):
            source, device = out_peer(k)
            return remote(
                across_buf.at[source], across_buf.at[source], send3.at[k], recv3.at[source], device
            )

        for k in range(1, inner):
            target, copy = scatter_to(k)

            @pl.when(target < chunks)
            def _():
                copy.start()

        @pl.when(my_in < chunks)
        def _():
            parts[my_in] = rs_send[mine_in]
            for k in range(1, inner):
                scatter_from(k).wait_recv()
            summed = parts[0].astype(f32)
            for source in range(1, inner):
                summed = summed + parts[source].astype(f32)
            if outer > 1:
                across_buf[my_out] = summed
                for k in range(1, outer):
                    across(k).start()
                for k in range(1, outer):
                    across_from(k).wait_recv()
                summed = across_buf[0]
                for source in range(1, outer):
                    summed = summed + across_buf[source]
                for k in range(1, outer):
                    across(k).wait_send()
            total[mine_in] = summed
            for k in range(1, inner):
                gather_to(k).start()
            forward_of(mine_in).start()

        for k in range(1, inner):
            source, at, copy = gather_from(k)

            @pl.when(source < chunks)
            def _():
                copy.wait_recv()
                forward_of(at).start()

    @pl.when(head == 1)
    def _():
        for index in range(chunks):
            forward_of(index).wait_recv()

    total_copy = pltpu.make_async_copy(total, total_hbm, out_sem.at[2])
    total_copy.start()

    each(groups - 1, lambda k: request_to(k).wait_send())
    each(groups - 1, lambda k: row_to(lax.rem(dp + 1 + k, groups)).wait_send())

    @pl.when(head == 0)
    def _():
        for k in range(1, inner):
            target, device = in_peer(k)

            @pl.when(target < chunks)
            def _():
                remote(
                    rs_send.at[0], parts.at[my_in], send1.at[k], recv1.at[my_in], device
                ).wait_send()

        @pl.when(my_in < chunks)
        def _():
            for k in range(1, inner):
                remote(
                    total.at[0], total.at[0], send2.at[k], recv2.at[0], in_peer(k)[1]
                ).wait_send()

        for index in range(chunks):
            forward_of(index).wait_send()

    out_copy.wait()
    grad_copy.wait()
    total_copy.wait()


def vmem(*shape, dtype=f32):
    return pltpu.VMEM(shape, dtype)


def run_layer(
    groups, ids, segments, valid, prompt, ag, fg, rel, cot, table, wqkv, wout, win, wdown
):
    share, width = cot.shape
    ff = 2 * win.shape[1]
    slot = 2 * share
    pairs = width // LANES
    rows = prompt.shape[0]
    ff_block = 768
    capacity = max(2, 2 * slot // (2 * groups))
    block = -(-capacity // 16) * 16
    inner = math.gcd(groups, 16)
    outer = groups // inner
    chunk_rows, chunk_cols = 16, width // 2
    chunks = 2 * -(-rows // chunk_rows)
    in_vmem = pl.BlockSpec(memory_space=pltpu.VMEM)
    in_smem = pl.BlockSpec(memory_space=pltpu.SMEM)
    in_hbm = pl.BlockSpec(memory_space=pl.ANY)
    dma = pltpu.SemaphoreType.DMA
    return pl.pallas_call(
        functools.partial(layer_kernel, groups, inner, block, rows),
        out_shape=(
            jax.ShapeDtypeStruct((share, width), bf16),
            jax.ShapeDtypeStruct((share, width), f32),
            jax.ShapeDtypeStruct((chunks, chunk_rows, chunk_cols), f32),
        ),
        in_specs=[in_vmem, in_vmem, in_smem] + [in_vmem] * 5 + [in_hbm] * 5,
        out_specs=[in_hbm] * 3,
        scratch_shapes=[
            vmem(*table.shape, dtype=bf16),
            vmem(3, width, width, dtype=bf16),
            vmem(width, width, dtype=bf16),
            vmem(width, ff, dtype=bf16),
            vmem(ff, width, dtype=bf16),
            vmem(groups, 1, LANES),
            vmem(groups, 1, LANES),
            vmem(groups, block, width, dtype=bf16),
            vmem(groups, block, width, dtype=bf16),
            vmem(2, 8, LANES),
            vmem(LANES, width),
            vmem(1, slot, dtype=jnp.int32),
            vmem(slot, LANES, dtype=bf16),
            vmem(share, LANES, dtype=bf16),
            vmem(share, width),
            vmem(LANES, width),
            vmem(ff // ff_block, share, ff_block),
            vmem(share, width, dtype=bf16),
            vmem(share, width),
            vmem(slot, width, dtype=bf16),
            vmem(slot, width, dtype=bf16),
            vmem(2, width, share, dtype=bf16),
            vmem(2, width, share, dtype=bf16),
            vmem(pairs, slot, LANES, dtype=bf16),
            vmem(2 * pairs, 5, LANES, LANES),
            vmem(pairs, slot, slot),
            vmem(width, share, dtype=bf16),
            vmem(share, width),
            vmem(share, width),
        ]
        + [vmem(pairs, share, LANES)] * 6
        + [
            vmem(pairs, slot, LANES, dtype=bf16),
            vmem(chunks, chunk_rows, chunk_cols, dtype=bf16),
            vmem(inner, chunk_rows, chunk_cols, dtype=bf16),
            vmem(outer, chunk_rows, chunk_cols),
            vmem(chunks, chunk_rows, chunk_cols),
            dma((5,)),
            dma((5,)),
            dma((5,)),
            dma((groups,)),
            dma((groups,)),
            dma((groups,)),
            dma((groups,)),
            dma((2,)),
            dma((2,)),
            dma((2, pairs)),
            dma((2, pairs)),
            dma((inner,)),
            dma((inner,)),
            dma((inner,)),
            dma((inner,)),
            dma((outer,)),
            dma((outer,)),
            dma((chunks,)),
            dma((chunks,)),
            dma((3,)),
        ],
        compiler_params=pltpu.CompilerParams(
            collective_id=1, has_side_effects=True, vmem_limit_bytes=60 * 2**20
        ),
        name="layer",
    )(ids, segments, valid, prompt, ag, fg, rel, cot, table, wqkv, wout, win, wdown)


def finish_kernel(
    clip_at, total_ref, prompt_ref, first_ref, second_ref, out_in, grad_in,
    out_ref, d_start_ref, grad_ref, norm_ref, new_ref, first_out_ref, second_out_ref, low_ref,
    sem,
):
    copies = [
        pltpu.make_async_copy(src, dst, sem.at[i])
        for i, (src, dst) in enumerate(((out_in, out_ref), (grad_in, d_start_ref)))
    ]
    for copy in copies:
        copy.start()
    rows = prompt_ref.shape[0]
    chunks = total_ref.shape[0]
    summed = jnp.concatenate(
        [
            jnp.concatenate([total_ref[c], total_ref[c + 1]], axis=1)
            for c in range(0, chunks, 2)
        ],
        axis=0,
    )[:rows]
    grad_ref[...] = summed
    norm = jnp.sqrt(jnp.sum(summed * summed, keepdims=True))
    norm_ref[...] = norm
    clipped = summed * jnp.minimum(1.0, clip_at / (norm + 1e-06))
    first_out = first_decay * first_ref[...] + (1.0 - first_decay) * clipped
    second_out = second_decay * second_ref[...] + (1.0 - second_decay) * clipped * clipped
    first_hat = first_out / (1.0 - first_decay**STEP)
    second_hat = second_out / (1.0 - second_decay**STEP)
    prompt = prompt_ref[...]
    new = prompt - learn_rate * (
        first_hat / (jnp.sqrt(second_hat) + adam_epsilon) + weight_decay * prompt
    )
    first_out_ref[...] = first_out
    second_out_ref[...] = second_out
    new_ref[...] = new
    low_ref[...] = new.astype(bf16)
    for copy in copies:
        copy.wait()


def run_finish(clip_at, total, prompt, first, second, out, grad):
    rows, width = prompt.shape
    shape = jax.ShapeDtypeStruct((rows, width), f32)
    in_vmem = pl.BlockSpec(memory_space=pltpu.VMEM)
    in_hbm = pl.BlockSpec(memory_space=pl.ANY)
    return pl.pallas_call(
        functools.partial(finish_kernel, clip_at),
        out_shape=(
            jax.ShapeDtypeStruct(out.shape, out.dtype),
            jax.ShapeDtypeStruct(grad.shape, grad.dtype),
            shape,
            jax.ShapeDtypeStruct((1, 1), f32),
            shape,
            shape,
            shape,
            jax.ShapeDtypeStruct((rows, width), bf16),
        ),
        in_specs=[in_vmem] * 4 + [in_hbm] * 2,
        out_specs=[in_hbm] * 2 + [in_vmem] * 6,
        scratch_shapes=[pltpu.SemaphoreType.DMA((2,))],
        compiler_params=pltpu.CompilerParams(vmem_limit_bytes=16 * 2**20),
        name="finish",
    )(total, prompt, first, second, out, grad)


def per_device(
    ids,
    segments,
    valid_rows,
    prompt,
    table,
    attn_gain,
    w_qkv,
    rel_bias,
    w_out,
    ff_gain,
    w_in,
    w_down,
    cotangent,
    first_moment,
    second_moment,
):
    groups = lax.axis_size("dp")
    rows, width = prompt.shape
    out, grad, total = run_layer(
        groups, ids, segments, valid_rows, prompt, attn_gain, ff_gain, rel_bias.T, cotangent,
        table, jnp.transpose(w_qkv, (1, 0, 2)), w_out, w_in, w_down,
    )
    clip_at = clip_share * math.sqrt(rows * width * groups)
    final, d_start, prompt_grad, norm, prompt_new, first_out, second_out, low = run_finish(
        clip_at, total, prompt, first_moment, second_moment, out, grad
    )
    return (final, d_start, prompt_grad, norm[0, 0], prompt_new, first_out, second_out, low)


def solution(mesh):
    in_specs = (
        P("dp", None),
        P("dp", None),
        P("dp"),
        P(),
        P("dp", None),
        P(),
        P(None, None, "head"),
        P(None, "head"),
        P("head", None),
        P(),
        P(None, "head"),
        P("head", None),
        P(("dp", "head"), None),
        P(),
        P(),
    )
    out_specs = (P(("dp", "head"), None), P(("dp", "head"), None), P(), P(), P(), P(), P(), P())
    return jax.shard_map(
        per_device, mesh=mesh, in_specs=in_specs, out_specs=out_specs, check_vma=False
    )
```

time: 146 us -> 76.9 us (0.53)
  the two profiles are of different devices: /device:TPU:1 before, /device:TPU:15 now
where the time goes in v2:
time: 76.9 us; the launch traced here: 76.7 us
  Pallas kernels  72 us (94%)
  local copies, waits for them, and re-layouts  3.11 us (4%)
  between operations  1.51 us (2%)
    pallas_call x1, Pallas kernels, run_layer(): pl.pallas_call(functools.partial(layer_kernel, groups, inner, block, rows...  69.9 us
    unnamed x12, local copies, waits for them, and re-layouts  3.11 us
    pallas_call x1, Pallas kernels, run_finish(): pl.pallas_call(functools.partial(finish_kernel, clip_at), out_shape=(jax....  2.14 us

profile of v2, /device:TPU:15, one launch (start us, length us, event | category | flops | bytes accessed | tf_op | source)
XLA Modules:
  0.0 76.7 jit_solution(1219705506883950967)
XLA Ops:
  1.3 0.0 copy-start
  1.3 0.0 copy-start.4
  1.3 0.0 copy-start.5
  1.3 69.9 %layer.1 = (bf16[256,768]{1,0:T(8,128)(2,1)}, f32[256,768]{1,0:T(8,128)}, f32[14,16,384]{2,1,0:T(8,128)}) custom-call(s32[1,512]{1,0:T(1,128)} %ids_ref.1, s32[1,412]{1,0:T(1,128)} %seg_ref.1, s32[1]{0:T(128)S(6)} %copy.23.valid_ref, f32[100,768]{1,0:T(8,128)} %prompt_ref.3, f32[768]{0:T(1024)} %ag_ref.1, f32[768]{0:T(1024)} %fg_ref.1, ...), custom_call_target="tpu_custom_call" | custom-call | tf_op jit(solution)/shard_map/layer/pallas_call | solution.py:594
  71.2 0.0 copy-done
  71.2 0.0 copy-done.4
  71.2 0.0 copy-done.5
  71.3 0.0 copy-start.1
  71.3 1.1 %copy-done.1 = f32[256,768]{1,0:T(8,128)S(1)} copy-done((f32[256,768]{1,0:T(8,128)S(1)}, f32[256,768]{1,0:T(8,128)}, u32[]{:S(2)}) %copy-start.1) | copy-done | bytes 786456
  72.4 0.0 copy-start.2
  72.4 1.0 %copy-done.2 = bf16[256,768]{1,0:T(8,128)(2,1)S(1)} copy-done((bf16[256,768]{1,0:T(8,128)(2,1)S(1)}, bf16[256,768]{1,0:T(8,128)(2,1)}, u32[]{:S(2)}) %copy-start.2) | copy-done | bytes 393240
  73.4 0.0 copy-start.3
  73.4 1.0 %copy-done.3 = f32[14,16,384]{2,1,0:T(8,128)S(1)} copy-done((f32[14,16,384]{2,1,0:T(8,128)S(1)}, f32[14,16,384]{2,1,0:T(8,128)}, u32[]{:S(2)}) %copy-start.3) | copy-done | bytes 344088
  74.4 2.1 %finish.1 = (bf16[256,768]{1,0:T(8,128)(2,1)}, f32[256,768]{1,0:T(8,128)}, f32[100,768]{1,0:T(8,128)}, f32[1,1]{1,0:T(1,128)}, f32[100,768]{1,0:T(8,128)}, /*ind...) custom-call(f32[14,16,384]{2,1,0:T(8,128)S(1)} %copy-done.3, f32[100,768]{1,0:T(8,128)S(1)} %copy-done, ...), custom_call_target="tpu_custom_call" | custom-call | tf_op jit(solution)/shard_map/finish/pallas_call | solution.py:714
Async XLA Ops:
  1.3 69.9 %copy-start = (f32[100,768]{1,0:T(8,128)S(1)}, f32[100,768]{1,0:T(8,128)}, u32[]{:S(2)}) copy-start(f32[100,768]{1,0:T(8,128)} %prompt_ref.3) | copy-start | bytes 921604
  1.3 69.9 %copy-start.4 = (f32[100,768]{1,0:T(8,128)S(1)}, f32[100,768]{1,0:T(8,128)}, u32[]{:S(2)}) copy-start(f32[100,768]{1,0:T(8,128)} %first_ref.1) | copy-start | bytes 921604
  1.3 69.9 %copy-start.5 = (f32[100,768]{1,0:T(8,128)S(1)}, f32[100,768]{1,0:T(8,128)}, u32[]{:S(2)}) copy-start(f32[100,768]{1,0:T(8,128)} %second_ref.1) | copy-start | bytes 921604
  71.3 1.1 %copy-start.1 = (f32[256,768]{1,0:T(8,128)S(1)}, f32[256,768]{1,0:T(8,128)}, u32[]{:S(2)}) copy-start(f32[256,768]{1,0:T(8,128)} %get-tuple-element.21.grad_in) | copy-start | bytes 2359300
  72.4 1.0 %copy-start.2 = (bf16[256,768]{1,0:T(8,128)(2,1)S(1)}, bf16[256,768]{1,0:T(8,128)(2,1)}, u32[]{:S(2)}) copy-start(bf16[256,768]{1,0:T(8,128)(2,1)} %get-tuple-element.20.out_in) | copy-start | bytes 1179652
  73.4 1.0 %copy-start.3 = (f32[14,16,384]{2,1,0:T(8,128)S(1)}, f32[14,16,384]{2,1,0:T(8,128)}, u32[]{:S(2)}) copy-start(f32[14,16,384]{2,1,0:T(8,128)} %get-tuple-element.19.total_ref) | copy-start | bytes 1032196

commit v3 on v2

--- a/solution.py
+++ b/solution.py
@@ -59,13 +59,13 @@
 
 def layer_kernel(
     groups, inner, block, rows,
-    ids_ref, seg_ref, valid_ref, prompt_ref, ag_ref, fg_ref, rel_ref, cot_ref,
-    table_hbm, wqkv_hbm, wout_hbm, win_hbm, wdown_hbm,
+    ids_ref, seg_ref, ag_ref, fg_ref, rel_ref, valid_ref,
+    prompt_hbm, cot_hbm, table_hbm, wqkv_hbm, wout_hbm, win_hbm, wdown_hbm,
     out_hbm, grad_hbm, total_hbm,
     table, wqkv, wout, win, wdown,
-    req_out, req_in, found, fetched, rel_all, prompt_pad, seg_pad, mask_k, mask_q,
-    x0, x0_prompt, d_act, out_buf, grad_buf,
-    k_all, v_all, kt, vt, qs, bias, probs, att_t, acc_out, acc_dn,
+    req_out, req_in, found, fetched, rel_all, prompt_in, prompt_pad, cot, seg_pad, seg_here, mask_k, mask_q,
+    x0, x0_prompt, d_act, act, d_scores, out_buf, grad_buf,
+    k_all, v_all, kt, vt, qs, bias, probs, att_t, acc_dn, out_low,
     dk_own, dv_own, dk_send, dv_send, dk_recv, dv_recv, dxb,
     rs_send, parts, across_buf, total,
     load_sem, far_send, far_recv, req_send, req_recv, row_send, row_recv,
@@ -95,6 +95,23 @@
             src, dst, send, recv, device_id=device, device_id_type=MESH
         )
 
+    barrier = pltpu.get_barrier_semaphore()
+
+    def peer_of(k):
+        if groups > 16:
+            return lax.rem(dp + 1 + k, groups)
+        flip, peer = groups - 1 - k, dp
+        for bit in range(groups.bit_length() - 1):
+            if flip >> bit & 1:
+                peer = peer + (1 - 2 * lax.rem(dp // (1 << bit), 2)) * (1 << bit)
+        return peer
+
+    def greet(k):
+        pl.semaphore_signal(barrier, inc=1, device_id=(peer_of(k), head), device_id_type=MESH)
+
+    each(groups - 1, greet)
+    pl.semaphore_signal(barrier, inc=1, device_id=other, device_id_type=MESH)
+
     my_cols = pl.ds(pl.multiple_of(head * half_width, half_width), half_width)
     my_ff = pl.ds(pl.multiple_of(head * half_ff, half_ff), half_ff)
     weight_pairs = (
@@ -103,27 +120,21 @@
         (wout_hbm, wout.at[my_cols, :]),
         (win_hbm, win.at[:, my_ff]),
     )
-    table_copy = pltpu.make_async_copy(table_hbm, table, load_sem.at[4])
+    cot_copy = pltpu.make_async_copy(cot_hbm, cot, load_sem.at[4])
+    cot_copy.start()
+    table_copy = pltpu.make_async_copy(table_hbm, table, load_sem.at[5])
     table_copy.start()
     local_copies = [
         pltpu.make_async_copy(src, dst, load_sem.at[i]) for i, (src, dst) in enumerate(weight_pairs)
     ]
     for copy in local_copies:
         copy.start()
+    prompt_copy = pltpu.make_async_copy(prompt_hbm, prompt_in, load_sem.at[6])
+    prompt_copy.start()
     far_copies = [
         remote(src, dst, far_send.at[i], far_recv.at[i], other)
         for i, (src, dst) in enumerate(weight_pairs)
     ]
-
-    barrier = pltpu.get_barrier_semaphore()
-
-    def greet(k):
-        pl.semaphore_signal(
-            barrier, inc=1, device_id=(lax.rem(dp + 1 + k, groups), head), device_id_type=MESH
-        )
-
-    pl.semaphore_signal(barrier, inc=1, device_id=other, device_id_type=MESH)
-    each(groups - 1, greet)
 
     lane = lax.broadcasted_iota(jnp.int32, (share, LANES), 1)
     row = lax.broadcasted_iota(jnp.int32, (share, LANES), 0) + head * share
@@ -157,9 +168,16 @@
     seg_pad[:, : seg_ref.shape[1]] = seg_ref[...]
     lanes_slot = lax.broadcasted_iota(jnp.int32, (1, slot), 1)
     seg_row = jnp.where(lanes_slot < rows, -1, pltpu.roll(seg_pad[...], rows, 1)).astype(f32)
+    seg_here[...] = seg_row
     limit = valid_ref[0] + rows
     square_lane = lax.broadcasted_iota(jnp.int32, (LANES, LANES), 1).astype(f32) - 1.0
     square_row = lax.broadcasted_iota(jnp.int32, (LANES, LANES), 0)
+    for qb in range(share // LANES):
+        spot = pl.ds(pl.multiple_of(head * share + qb * LANES, LANES), LANES)
+        seg_col = jnp.broadcast_to(seg_here[:, spot], (LANES, LANES)).T
+        mask_q[qb * LANES : (qb + 1) * LANES, :] = (
+            (seg_col == square_lane).astype(f32).astype(bf16)
+        )
     for kb in range(slot // LANES):
         at = kb * LANES
         seg_col = jnp.broadcast_to(seg_row[:, at : at + LANES], (LANES, LANES)).T
@@ -168,24 +186,21 @@
         allowed = (key < rows) | (same & (key < limit))
         mask_k[at : at + LANES, :] = jnp.where(allowed, 0.0, masked_score).astype(bf16)
 
-        @pl.when(head == at // share)
-        def _():
-            mask_q[at % share : at % share + LANES, :] = same.astype(f32).astype(bf16)
-
     live = row[:, :1] < limit
-    dy = jnp.where(live, cot_ref[...].astype(f32), 0.0).astype(bf16)
+    cot_copy.wait()
+    dy = jnp.where(live, cot[...].astype(f32), 0.0).astype(bf16)
 
     pl.semaphore_wait(barrier, groups)
     req_in[dp] = req_out[dp]
 
     def request_to(k):
-        peer = lax.rem(dp + 1 + k, groups)
+        peer = peer_of(k)
         return remote(
             req_out.at[peer], req_in.at[dp], req_send.at[peer], req_recv.at[dp], (peer, head)
         )
 
     def request_from(k):
-        peer = lax.rem(dp + 1 + k, groups)
+        peer = peer_of(k)
         return remote(
             req_out.at[peer], req_in.at[peer], req_send.at[peer], req_recv.at[peer], (peer, head)
         )
@@ -211,7 +226,11 @@
     table_copy.wait()
     each(groups - 1, lambda k: request_from(k).wait_recv())
     vocab_lane = lax.broadcasted_iota(jnp.int32, (block, vocab), 1).astype(f32)
-    bunch = 8
+    bunch = max(4, groups // 16)
+    bunches = groups // bunch
+    half_bunches = bunches // 2
+    half_groups = groups // 2
+    side_of = dp // half_groups
 
     def row_to(peer):
         return remote(
@@ -224,7 +243,8 @@
         )
 
     def serve(g):
-        base = lax.rem(dp // bunch + 1 + g, groups // bunch) * bunch
+        side = jnp.where(g < half_bunches, 1 - side_of, side_of)
+        base = (side * half_bunches + lax.rem(g, half_bunches)) * bunch
         wants = jnp.concatenate(
             [req_in[base + j] for j in range(bunch)] + [jnp.zeros((LANES - bunch, LANES), f32)],
             axis=0,
@@ -244,14 +264,14 @@
             def _():
                 row_to(base + j).start()
 
-    each(groups // bunch, serve)
+    each(bunches, serve)
     fetched[dp] = found[dp]
 
-    @pl.when(head == 0)
-    def _():
-        prompt_pad[...] = jnp.zeros_like(prompt_pad)
-        prompt_pad[:rows, :] = prompt_ref[...]
-        x0_prompt[...] = dot(order, prompt_pad[...], NN, exact_mode)
+    prompt_copy.wait()
+
+    prompt_pad[...] = jnp.zeros_like(prompt_pad)
+    prompt_pad[:rows, :] = prompt_in[...]
+    x0_prompt[...] = dot(order, prompt_pad[...], NN, exact_mode)
 
     rel_copy.wait()
     spread = lax.broadcasted_iota(jnp.int32, (1, 2 * LANES), 1)
@@ -280,21 +300,29 @@
         copy.wait()
     far_copies[1].wait()
 
-    for peer in range(groups) if groups <= 16 else ():
+    spot_lane = lax.broadcasted_iota(jnp.int32, (share, half_groups * block), 1).astype(f32)
+
+    def rows_of(side):
+        base = side * half_groups
+        take = (place - (base * block).astype(f32) == spot_lane).astype(f32).astype(bf16)
+        return dot(
+            take, fetched[pl.ds(base, half_groups)].reshape(half_groups * block, width)
+        )
+
+    def near_wait(j):
+        peer = side_of * half_groups + j
 
         @pl.when(peer != dp)
         def _():
             row_from(peer).wait_recv()
 
-    if groups > 16:
-        each(groups - 1, lambda k: row_from(lax.rem(dp + 1 + k, groups)).wait_recv())
-    spot_lane = lax.broadcasted_iota(jnp.int32, (share, spots), 1).astype(f32)
-    take = (place == spot_lane).astype(f32).astype(bf16)
-    x0[...] = dot(take, fetched[...].reshape(spots, width))
-
-    @pl.when(head == 0)
-    def _():
-        x0[:LANES, :] = x0[:LANES, :] + x0_prompt[...]
+    each(half_groups, near_wait)
+    near_rows = rows_of(side_of)
+    x0[...] = near_rows
+    x0[:LANES, :] = near_rows[:LANES] + x0_prompt[...]
+
+    each(half_groups, lambda j: row_from((1 - side_of) * half_groups + j).wait_recv())
+    x0[...] = x0[...] + rows_of(1 - side_of)
 
     attn_gain = ag_ref[...].reshape(1, width)
     ff_gain = fg_ref[...].reshape(1, width)
@@ -354,12 +382,12 @@
             ).astype(bf16)
         return carry
 
-    lax.fori_loop(0, pairs, forward, 0)
+    lax.fori_loop(0, pairs, forward, 0, unroll=True)
     far_copies[2].wait()
     x1 = x0[...] + dot(att_t[...].T, wout[...])
     n2 = rms_scale(x1, ff_gain).astype(bf16)
     far_copies[3].wait()
-    acc_out[...] = x1
+    out_buf[...] = x1
     acc_dn[...] = jnp.zeros_like(acc_dn)
 
     def feed(i, carry):
@@ -367,19 +395,15 @@
         u = dot(n2, win[:, at])
         square = u * u
         t = jnp.tanh(GELU_C * (u + 0.044715 * (u * square)))
-        active = (0.5 * u * (1.0 + t)).astype(bf16)
+        act[i] = (0.5 * u * (1.0 + t)).astype(bf16)
         slope = 0.5 * (1.0 + t) + 0.5 * u * (1.0 - t * t) * (
             GELU_C * (1.0 + 3 * 0.044715 * square)
         )
         d_hidden = (d_act[i] * slope).astype(bf16)
-        acc_out[...] += dot(active, wdown[at, :])
         acc_dn[...] += dot(d_hidden, win[:, at], NT)
         return carry
 
-    lax.fori_loop(0, ff // ff_block, feed, 0)
-    out_buf[...] = acc_out[...].astype(bf16)
-    out_copy = pltpu.make_async_copy(out_buf, out_hbm, out_sem.at[0])
-    out_copy.start()
+    lax.fori_loop(0, ff // ff_block, feed, 0, unroll=True)
     dx1 = dy.astype(f32) + rms_back(x1, ff_gain, acc_dn[...])
     grad_buf[...] = dx1
     d_att = dot(dx1.astype(bf16), wout[...], NT).astype(bf16)
@@ -393,6 +417,15 @@
             remote(src.at[p], dst.at[p], dkv_send.at[i, p], dkv_recv.at[i, p], other)
             for i, (src, dst) in enumerate(((dk_send, dk_recv), (dv_send, dv_recv)))
         ]
+
+    def query_grad(p, d_score, begin, end):
+        half = LANES // 2
+        for a in range(2):
+            side = d_score[:, a * share + begin : a * share + end]
+            feat = pl.ds(pl.multiple_of(p * LANES + a * half, half), half)
+            att_t[feat, begin:end] = (
+                (dot(kt[0, feat, :], side[:share]) + dot(kt[1, feat, :], side[share:])) * 0.125
+            ).astype(bf16)
 
     def backward(p, carry):
         cols = pl.ds(pl.multiple_of(p * LANES, LANES), LANES)
@@ -402,13 +435,8 @@
         delta = jnp.sum(prob * d_prob, axis=0, keepdims=True)
         d_score = (prob * (d_prob - delta)).astype(bf16)
         low = prob.astype(bf16)
-        half = LANES // 2
-        for a in range(2):
-            side = d_score[:, a * share : (a + 1) * share]
-            feat = pl.ds(pl.multiple_of(p * LANES + a * half, half), half)
-            att_t[feat, :] = (
-                (dot(kt[0, feat, :], side[:share]) + dot(kt[1, feat, :], side[share:])) * 0.125
-            ).astype(bf16)
+        d_scores[p] = d_score
+        query_grad(p, d_score, 0, LANES)
         d_v = dot(low, d_out)
         d_k = dot(d_score, qs[p])
         first = head == 0
@@ -420,17 +448,24 @@
             copy.start()
         return carry
 
-    lax.fori_loop(0, pairs, backward, 0)
-    acc_dn[...] = dot(att_t[...].T, wqkv[0], NT)
+    lax.fori_loop(0, pairs, backward, 0, unroll=True)
+
+    def input_grad(part):
+        d_k = jnp.concatenate(
+            [(dk_own[p, part] + dk_recv[p, part]).astype(bf16) for p in range(pairs)], axis=1
+        )
+        d_v = jnp.concatenate(
+            [(dv_own[p, part] + dv_recv[p, part]).astype(bf16) for p in range(pairs)], axis=1
+        )
+        d_n1 = acc_dn[part] + dot(d_k, wqkv[1], NT) + dot(d_v, wqkv[2], NT)
+        grad_buf[part] = grad_buf[part] + rms_back(x0[part], attn_gain, d_n1)
+
+    first_rows, last_rows = slice(0, LANES), slice(LANES, share)
+    acc_dn[first_rows] = dot(att_t[:, first_rows].T, wqkv[0], NT)
     for p in range(pairs):
         for copy in send_of(p):
             copy.wait()
-    d_k = jnp.concatenate([(dk_own[p] + dk_recv[p]).astype(bf16) for p in range(pairs)], axis=1)
-    d_v = jnp.concatenate([(dv_own[p] + dv_recv[p]).astype(bf16) for p in range(pairs)], axis=1)
-    d_n1 = acc_dn[...] + dot(d_k, wqkv[1], NT) + dot(d_v, wqkv[2], NT)
-    grad_buf[...] = grad_buf[...] + rms_back(x0[...], attn_gain, d_n1)
-    grad_copy = pltpu.make_async_copy(grad_buf, grad_hbm, out_sem.at[1])
-    grad_copy.start()
+    input_grad(first_rows)
 
     chunks, chunk_rows, chunk_cols = total.shape
 
@@ -440,58 +475,56 @@
         )
 
     def in_peer(k):
-        target = lax.rem(my_in + k, inner)
+        target, flip = my_in, inner - k
+        for bit in range(inner.bit_length() - 1):
+            if flip >> bit & 1:
+                target = target + (1 - 2 * lax.rem(my_in // (1 << bit), 2)) * (1 << bit)
         return target, (my_out * inner + target, head)
 
     def out_peer(k):
         target = lax.rem(my_out + k, outer)
         return target, (target * inner + my_in, head)
 
+    mine_in = jnp.minimum(my_in, chunks - 1)
+
+    def scatter_to(k):
+        target, device = in_peer(k)
+        at = jnp.minimum(target, chunks - 1)
+        return target, remote(rs_send.at[at], parts.at[my_in], send1.at[k], recv1.at[my_in], device)
+
+    def scatter_from(k):
+        source, device = in_peer(k)
+        return remote(rs_send.at[0], parts.at[source], send1.at[k], recv1.at[source], device)
+
+    def gather_to(k):
+        return remote(
+            total.at[mine_in], total.at[mine_in], send2.at[k], recv2.at[mine_in], in_peer(k)[1]
+        )
+
+    def gather_from(k):
+        source, device = in_peer(k)
+        at = jnp.minimum(source, chunks - 1)
+        return source, at, remote(total.at[at], total.at[at], send2.at[k], recv2.at[at], device)
+
+    def across(k):
+        return remote(
+            across_buf.at[my_out], across_buf.at[my_out], send3.at[k], recv3.at[my_out],
+            out_peer(k)[1],
+        )
+
+    def across_from(k):
+        source, device = out_peer(k)
+        return remote(
+            across_buf.at[source], across_buf.at[source], send3.at[k], recv3.at[source], device
+        )
+
     @pl.when(head == 0)
     def _():
-        local = dot(order, grad_buf[:LANES, :], TN, exact_mode).astype(bf16)
+        local = dot(order, grad_buf[first_rows], TN, exact_mode).astype(bf16)
         for c in range(chunks):
             top, left = (c // 2) * chunk_rows, (c % 2) * chunk_cols
             rs_send[c] = local[top : top + chunk_rows, left : left + chunk_cols]
 
-        def scatter_to(k):
-            target, device = in_peer(k)
-            return target, remote(
-                rs_send.at[jnp.minimum(target, chunks - 1)], parts.at[my_in], send1.at[k], recv1.at[my_in], device
-            )
-
-        def scatter_from(k):
-            source, device = in_peer(k)
-            return remote(
-                rs_send.at[0], parts.at[source], send1.at[k], recv1.at[source], device
-            )
-
-        mine_in = jnp.minimum(my_in, chunks - 1)
-
-        def gather_to(k):
-            return remote(
-                total.at[mine_in], total.at[mine_in], send2.at[k], recv2.at[mine_in], in_peer(k)[1]
-            )
-
-        def gather_from(k):
-            source, device = in_peer(k)
-            at = jnp.minimum(source, chunks - 1)
-            return source, at, remote(
-                total.at[at], total.at[at], send2.at[k], recv2.at[at], device
-            )
-
-        def across(k):
-            return remote(
-                across_buf.at[my_out], across_buf.at[my_out], send3.at[k], recv3.at[my_out],
-                out_peer(k)[1],
-            )
-
-        def across_from(k):
-            source, device = out_peer(k)
-            return remote(
-                across_buf.at[source], across_buf.at[source], send3.at[k], recv3.at[source], device
-            )
-
         for k in range(1, inner):
             target, copy = scatter_to(k)
 
@@ -499,30 +532,45 @@
             def _():
                 copy.start()
 
-        @pl.when(my_in < chunks)
-        def _():
-            parts[my_in] = rs_send[mine_in]
-            for k in range(1, inner):
-                scatter_from(k).wait_recv()
-            summed = parts[0].astype(f32)
-            for source in range(1, inner):
-                summed = summed + parts[source].astype(f32)
-            if outer > 1:
-                across_buf[my_out] = summed
-                for k in range(1, outer):
-                    across(k).start()
-                for k in range(1, outer):
-                    across_from(k).wait_recv()
-                summed = across_buf[0]
-                for source in range(1, outer):
-                    summed = summed + across_buf[source]
-                for k in range(1, outer):
-                    across(k).wait_send()
-            total[mine_in] = summed
-            for k in range(1, inner):
-                gather_to(k).start()
-            forward_of(mine_in).start()
-
+    for p in range(pairs):
+        query_grad(p, d_scores[p], LANES, share)
+    for i in range(ff // ff_block):
+        out_buf[...] = out_buf[...] + dot(act[i], wdown[i * ff_block : (i + 1) * ff_block, :])
+    out_low[...] = out_buf[...].astype(bf16)
+    out_copy = pltpu.make_async_copy(out_low, out_hbm, out_sem.at[0])
+    out_copy.start()
+
+    @pl.when((head == 0) & (my_in < chunks))
+    def _():
+        parts[my_in] = rs_send[mine_in]
+        for k in range(1, inner):
+            scatter_from(k).wait_recv()
+        summed = parts[0].astype(f32)
+        for source in range(1, inner):
+            summed = summed + parts[source].astype(f32)
+        if outer > 1:
+            across_buf[my_out] = summed
+            for k in range(1, outer):
+                across(k).start()
+            for k in range(1, outer):
+                across_from(k).wait_recv()
+            summed = across_buf[0]
+            for source in range(1, outer):
+                summed = summed + across_buf[source]
+            for k in range(1, outer):
+                across(k).wait_send()
+        total[mine_in] = summed.astype(bf16)
+        for k in range(1, inner):
+            gather_to(k).start()
+        forward_of(mine_in).start()
+
+    acc_dn[last_rows] = dot(att_t[:, last_rows].T, wqkv[0], NT)
+    input_grad(last_rows)
+    grad_copy = pltpu.make_async_copy(grad_buf, grad_hbm, out_sem.at[1])
+    grad_copy.start()
+
+    @pl.when(head == 0)
+    def _():
         for k in range(1, inner):
             source, at, copy = gather_from(k)
 
@@ -540,7 +588,7 @@
     total_copy.start()
 
     each(groups - 1, lambda k: request_to(k).wait_send())
-    each(groups - 1, lambda k: row_to(lax.rem(dp + 1 + k, groups)).wait_send())
+    each(groups - 1, lambda k: row_to(peer_of(k)).wait_send())
 
     @pl.when(head == 0)
     def _():
@@ -549,16 +597,12 @@
 
             @pl.when(target < chunks)
             def _():
-                remote(
-                    rs_send.at[0], parts.at[my_in], send1.at[k], recv1.at[my_in], device
-                ).wait_send()
+                scatter_to(k)[1].wait_send()
 
         @pl.when(my_in < chunks)
         def _():
             for k in range(1, inner):
-                remote(
-                    total.at[0], total.at[0], send2.at[k], recv2.at[0], in_peer(k)[1]
-                ).wait_send()
+                gather_to(k).wait_send()
 
         for index in range(chunks):
             forward_of(index).wait_send()
@@ -573,7 +617,7 @@
 
 
 def run_layer(
-    groups, ids, segments, valid, prompt, ag, fg, rel, cot, table, wqkv, wout, win, wdown
+    groups, ids, segments, ag, fg, rel, valid, prompt, cot, table, wqkv, wout, win, wdown
 ):
     share, width = cot.shape
     ff = 2 * win.shape[1]
@@ -588,7 +632,6 @@
     chunk_rows, chunk_cols = 16, width // 2
     chunks = 2 * -(-rows // chunk_rows)
     in_vmem = pl.BlockSpec(memory_space=pltpu.VMEM)
-    in_smem = pl.BlockSpec(memory_space=pltpu.SMEM)
     in_hbm = pl.BlockSpec(memory_space=pl.ANY)
     dma = pltpu.SemaphoreType.DMA
     return pl.pallas_call(
@@ -596,9 +639,9 @@
         out_shape=(
             jax.ShapeDtypeStruct((share, width), bf16),
             jax.ShapeDtypeStruct((share, width), f32),
-            jax.ShapeDtypeStruct((chunks, chunk_rows, chunk_cols), f32),
+            jax.ShapeDtypeStruct((chunks, chunk_rows, chunk_cols), bf16),
         ),
-        in_specs=[in_vmem, in_vmem, in_smem] + [in_vmem] * 5 + [in_hbm] * 5,
+        in_specs=[in_vmem] * 5 + [pl.BlockSpec(memory_space=pltpu.SMEM)] + [in_hbm] * 7,
         out_specs=[in_hbm] * 3,
         scratch_shapes=[
             vmem(*table.shape, dtype=bf16),
@@ -611,14 +654,19 @@
             vmem(groups, block, width, dtype=bf16),
             vmem(groups, block, width, dtype=bf16),
             vmem(2, 8, LANES),
+            vmem(rows, width),
             vmem(LANES, width),
+            vmem(share, width, dtype=bf16),
             vmem(1, slot, dtype=jnp.int32),
+            vmem(1, slot),
             vmem(slot, LANES, dtype=bf16),
             vmem(share, LANES, dtype=bf16),
             vmem(share, width),
             vmem(LANES, width),
             vmem(ff // ff_block, share, ff_block),
-            vmem(share, width, dtype=bf16),
+            vmem(ff // ff_block, share, ff_block, dtype=bf16),
+            vmem(pairs, slot, slot, dtype=bf16),
+            vmem(share, width),
             vmem(share, width),
             vmem(slot, width, dtype=bf16),
             vmem(slot, width, dtype=bf16),
@@ -629,7 +677,7 @@
             vmem(pairs, slot, slot),
             vmem(width, share, dtype=bf16),
             vmem(share, width),
-            vmem(share, width),
+            vmem(share, width, dtype=bf16),
         ]
         + [vmem(pairs, share, LANES)] * 6
         + [
@@ -637,8 +685,8 @@
             vmem(chunks, chunk_rows, chunk_cols, dtype=bf16),
             vmem(inner, chunk_rows, chunk_cols, dtype=bf16),
             vmem(outer, chunk_rows, chunk_cols),
-            vmem(chunks, chunk_rows, chunk_cols),
-            dma((5,)),
+            vmem(chunks, chunk_rows, chunk_cols, dtype=bf16),
+            dma((7,)),
             dma((5,)),
             dma((5,)),
             dma((groups,)),
@@ -663,53 +711,79 @@
             collective_id=1, has_side_effects=True, vmem_limit_bytes=60 * 2**20
         ),
         name="layer",
-    )(ids, segments, valid, prompt, ag, fg, rel, cot, table, wqkv, wout, win, wdown)
+    )(ids, segments, ag, fg, rel, valid, prompt, cot, table, wqkv, wout, win, wdown)
 
 
 def finish_kernel(
-    clip_at, total_ref, prompt_ref, first_ref, second_ref, out_in, grad_in,
-    out_ref, d_start_ref, grad_ref, norm_ref, new_ref, first_out_ref, second_out_ref, low_ref,
-    sem,
+    clip_at, prompt_hbm, first_hbm, second_hbm, total_hbm, out_hbm, grad_hbm,
+    *refs,
 ):
-    copies = [
-        pltpu.make_async_copy(src, dst, sem.at[i])
-        for i, (src, dst) in enumerate(((out_in, out_ref), (grad_in, d_start_ref)))
+    results, (prompt_ref, first_ref, second_ref, total_ref, out_buf, grad_buf), (
+        grad_ref, norm_ref, new_ref, first_out_ref, second_out_ref, low_ref,
+    ), (load_sem, store_sem) = refs[:8], refs[8:14], refs[14:20], refs[20:]
+    loads = [
+        pltpu.make_async_copy(src, dst, load_sem.at[i])
+        for i, (src, dst) in enumerate(
+            (
+                (total_hbm, total_ref), (first_hbm, first_ref), (second_hbm, second_ref),
+                (prompt_hbm, prompt_ref), (out_hbm, out_buf), (grad_hbm, grad_buf),
+            )
+        )
     ]
-    for copy in copies:
+    for copy in loads:
         copy.start()
+    stores = []
+
+    def store(src, index):
+        stores.append(pltpu.make_async_copy(src, results[index], store_sem.at[index]))
+        stores[-1].start()
+
     rows = prompt_ref.shape[0]
     chunks = total_ref.shape[0]
+    loads[0].wait()
     summed = jnp.concatenate(
         [
             jnp.concatenate([total_ref[c], total_ref[c + 1]], axis=1)
             for c in range(0, chunks, 2)
         ],
         axis=0,
-    )[:rows]
+    ).astype(f32)[:rows]
     grad_ref[...] = summed
+    store(grad_ref, 2)
     norm = jnp.sqrt(jnp.sum(summed * summed, keepdims=True))
     norm_ref[...] = norm
+    store(norm_ref, 3)
     clipped = summed * jnp.minimum(1.0, clip_at / (norm + 1e-06))
+    loads[1].wait()
     first_out = first_decay * first_ref[...] + (1.0 - first_decay) * clipped
+    first_out_ref[...] = first_out
+    store(first_out_ref, 5)
+    loads[2].wait()
     second_out = second_decay * second_ref[...] + (1.0 - second_decay) * clipped * clipped
+    second_out_ref[...] = second_out
+    store(second_out_ref, 6)
+    loads[4].wait()
+    store(out_buf, 0)
+    loads[5].wait()
+    store(grad_buf, 1)
     first_hat = first_out / (1.0 - first_decay**STEP)
     second_hat = second_out / (1.0 - second_decay**STEP)
+    loads[3].wait()
     prompt = prompt_ref[...]
     new = prompt - learn_rate * (
         first_hat / (jnp.sqrt(second_hat) + adam_epsilon) + weight_decay * prompt
     )
-    first_out_ref[...] = first_out
-    second_out_ref[...] = second_out
     new_ref[...] = new
+    store(new_ref, 4)
     low_ref[...] = new.astype(bf16)
-    for copy in copies:
+    store(low_ref, 7)
+    for copy in stores:
         copy.wait()
 
 
 def run_finish(clip_at, total, prompt, first, second, out, grad):
     rows, width = prompt.shape
     shape = jax.ShapeDtypeStruct((rows, width), f32)
-    in_vmem = pl.BlockSpec(memory_space=pltpu.VMEM)
     in_hbm = pl.BlockSpec(memory_space=pl.ANY)
     return pl.pallas_call(
         functools.partial(finish_kernel, clip_at),
@@ -723,12 +797,27 @@
             shape,
             jax.ShapeDtypeStruct((rows, width), bf16),
         ),
-        in_specs=[in_vmem] * 4 + [in_hbm] * 2,
-        out_specs=[in_hbm] * 2 + [in_vmem] * 6,
-        scratch_shapes=[pltpu.SemaphoreType.DMA((2,))],
-        compiler_params=pltpu.CompilerParams(vmem_limit_bytes=16 * 2**20),
+        in_specs=[in_hbm] * 6,
+        out_specs=[in_hbm] * 8,
+        scratch_shapes=[
+            vmem(rows, width),
+            vmem(rows, width),
+            vmem(rows, width),
+            vmem(*total.shape, dtype=bf16),
+            vmem(*out.shape, dtype=bf16),
+            vmem(*grad.shape),
+            vmem(rows, width),
+            vmem(1, 1),
+            vmem(rows, width),
+            vmem(rows, width),
+            vmem(rows, width),
+            vmem(rows, width, dtype=bf16),
+            pltpu.SemaphoreType.DMA((6,)),
+            pltpu.SemaphoreType.DMA((8,)),
+        ],
+        compiler_params=pltpu.CompilerParams(vmem_limit_bytes=63 * 2**20),
         name="finish",
-    )(total, prompt, first, second, out, grad)
+    )(prompt, first, second, total, out, grad)
 
 
 def per_device(
@@ -751,8 +840,8 @@
     groups = lax.axis_size("dp")
     rows, width = prompt.shape
     out, grad, total = run_layer(
-        groups, ids, segments, valid_rows, prompt, attn_gain, ff_gain, rel_bias.T, cotangent,
-        table, jnp.transpose(w_qkv, (1, 0, 2)), w_out, w_in, w_down,
+        groups, ids, segments, attn_gain, ff_gain, rel_bias.T, valid_rows, prompt, cotangent, table,
+        jnp.transpose(w_qkv, (1, 0, 2)), w_out, w_in, w_down,
     )
     clip_at = clip_share * math.sqrt(rows * width * groups)
     final, d_start, prompt_grad, norm, prompt_new, first_out, second_out, low = run_finish(

time: 76.9 us -> 68.5 us (0.89)
  the two profiles are of different devices: /device:TPU:15 before, /device:TPU:1 now
where the time goes in v3:
time: 68.5 us; the launch traced here: 68.3 us
  Pallas kernels  66.8 us (98%)
  between operations  1.45 us (2%)
    pallas_call x1, Pallas kernels, run_layer(): pl.pallas_call(functools.partial(layer_kernel, groups, inner, block, rows...  64 us
    pallas_call x1, Pallas kernels, run_finish(): pl.pallas_call(functools.partial(finish_kernel, clip_at), out_shape=(jax....  2.79 us

profile of v3, /device:TPU:1, one launch (start us, length us, event | category | flops | bytes accessed | tf_op | source)
XLA Modules:
  0.0 68.3 jit_solution(7175344428657818961)
XLA Ops:
  1.3 64.0 %layer.1 = (bf16[256,768]{1,0:T(8,128)(2,1)}, f32[256,768]{1,0:T(8,128)}, bf16[14,16,384]{2,1,0:T(8,128)(2,1)}) custom-call(s32[1,512]{1,0:T(1,128)} %ids_ref.1, s32[1,412]{1,0:T(1,128)} %seg_ref.1, f32[768]{0:T(1024)} %ag_ref.1, f32[768]{0:T(1024)} %fg_ref.1, bf16[6,32]{1,0:T(8,128)(2,1)} %bitcast.4, s32[1]{0:T(128)S(6)} %copy.23.valid_ref, ...), custom_call_target="tpu_custom_call" | custom-call | tf_op jit(solution)/shard_map/layer/pallas_call | solution.py:637
  65.3 2.8 %finish.1 = (bf16[256,768]{1,0:T(8,128)(2,1)}, f32[256,768]{1,0:T(8,128)}, f32[100,768]{1,0:T(8,128)}, f32[1,1]{1,0:T(1,128)}, f32[100,768]{1,0:T(8,128)}, /*ind...) custom-call(f32[100,768]{1,0:T(8,128)} %prompt_hbm.3, f32[100,768]{1,0:T(8,128)} %first_hbm.1, ...), custom_call_target="tpu_custom_call" | custom-call | tf_op jit(solution)/shard_map/finish/pallas_call | solution.py:788

commit v4 on v3

--- a/solution.py
+++ b/solution.py
@@ -59,9 +59,9 @@
 
 def layer_kernel(
     groups, inner, block, rows,
-    ids_ref, seg_ref, ag_ref, fg_ref, rel_ref, valid_ref,
-    prompt_hbm, cot_hbm, table_hbm, wqkv_hbm, wout_hbm, win_hbm, wdown_hbm,
+    valid_ref, ids_hbm, seg_hbm, ag_hbm, fg_hbm, rel_hbm, prompt_hbm, cot_hbm, table_hbm, wqkv_hbm, wout_hbm, win_hbm, wdown_hbm,
     out_hbm, grad_hbm, total_hbm,
+    ids_ref, seg_ref, ag_ref, fg_ref, rel_ref,
     table, wqkv, wout, win, wdown,
     req_out, req_in, found, fetched, rel_all, prompt_in, prompt_pad, cot, seg_pad, seg_here, mask_k, mask_q,
     x0, x0_prompt, d_act, act, d_scores, out_buf, grad_buf,
@@ -88,7 +88,6 @@
     my_in = lax.rem(dp, inner)
     my_out = dp // inner
     mine = pl.ds(pl.multiple_of(head * share, share), share)
-    theirs = pl.ds(pl.multiple_of((1 - head) * share, share), share)
 
     def remote(src, dst, send, recv, device):
         return pltpu.make_async_remote_copy(
@@ -112,6 +111,17 @@
     each(groups - 1, greet)
     pl.semaphore_signal(barrier, inc=1, device_id=other, device_id_type=MESH)
 
+    small_copies = [
+        pltpu.make_async_copy(src, dst, load_sem.at[7 + i])
+        for i, (src, dst) in enumerate(
+            (
+                (ids_hbm, ids_ref), (seg_hbm, seg_ref), (rel_hbm, rel_ref), (ag_hbm, ag_ref),
+                (fg_hbm, fg_ref),
+            )
+        )
+    ]
+    for copy in small_copies:
+        copy.start()
     my_cols = pl.ds(pl.multiple_of(head * half_width, half_width), half_width)
     my_ff = pl.ds(pl.multiple_of(head * half_ff, half_ff), half_ff)
     weight_pairs = (
@@ -139,6 +149,7 @@
     lane = lax.broadcasted_iota(jnp.int32, (share, LANES), 1)
     row = lax.broadcasted_iota(jnp.int32, (share, LANES), 0) + head * share
     lane_f = lane.astype(f32)
+    small_copies[0].wait()
     row_ids = ids_ref[:, mine].astype(f32)
     ids_col = jnp.concatenate(
         [
@@ -162,9 +173,11 @@
 
     order = jnp.where(is_text[:LANES], 0.0, (ids_col[:LANES] == lane_f[:LANES]).astype(f32))
 
+    small_copies[2].wait()
     rel_all[head] = jnp.zeros((8, LANES), f32)
     rel_all[head, : rel_ref.shape[0], : rel_ref.shape[1]] = rel_ref[...].astype(f32)
 
+    small_copies[1].wait()
     seg_pad[:, : seg_ref.shape[1]] = seg_ref[...]
     lanes_slot = lax.broadcasted_iota(jnp.int32, (1, slot), 1)
     seg_row = jnp.where(lanes_slot < rows, -1, pltpu.roll(seg_pad[...], rows, 1)).astype(f32)
@@ -184,7 +197,7 @@
         same = seg_col == square_lane
         key = square_row + at
         allowed = (key < rows) | (same & (key < limit))
-        mask_k[at : at + LANES, :] = jnp.where(allowed, 0.0, masked_score).astype(bf16)
+        mask_k[at // share, at % share : at % share + LANES, :] = jnp.where(allowed, 0.0, masked_score).astype(bf16)
 
     live = row[:, :1] < limit
     cot_copy.wait()
@@ -324,65 +337,82 @@
     each(half_groups, lambda j: row_from((1 - side_of) * half_groups + j).wait_recv())
     x0[...] = x0[...] + rows_of(1 - side_of)
 
+    small_copies[3].wait()
+    small_copies[4].wait()
     attn_gain = ag_ref[...].reshape(1, width)
     ff_gain = fg_ref[...].reshape(1, width)
     n1 = rms_scale(x0[...], attn_gain).astype(bf16)
-    k_all[mine, :] = dot(n1, wqkv[1]).astype(bf16)
-    k_copy = remote(
-        k_all.at[mine, :], k_all.at[mine, :], kv_send.at[0], kv_recv.at[0], other
-    )
+    k_all[head] = dot(n1, wqkv[1]).astype(bf16)
+    k_copy = remote(k_all.at[head], k_all.at[head], kv_send.at[0], kv_recv.at[0], other)
     k_copy.start()
-    v_all[mine, :] = dot(n1, wqkv[2]).astype(bf16)
-    v_copy = remote(
-        v_all.at[mine, :], v_all.at[mine, :], kv_send.at[1], kv_recv.at[1], other
-    )
+    v_all[head] = dot(n1, wqkv[2]).astype(bf16)
+    v_copy = remote(v_all.at[head], v_all.at[head], kv_send.at[1], kv_recv.at[1], other)
     v_copy.start()
     q = dot(n1, wqkv[0]).astype(bf16) * jnp.asarray(0.125, bf16)
     for p in range(pairs):
         part = q[:, p * LANES : (p + 1) * LANES]
         qs[p, :share, :] = jnp.where(lane < LANES // 2, part, jnp.zeros_like(part))
         qs[p, share:, :] = jnp.where(lane >= LANES // 2, part, jnp.zeros_like(part))
-    kt[head] = k_all[mine, :].T
-    vt[head] = v_all[mine, :].T
-    k_copy.wait()
-    kt[1 - head] = k_all[theirs, :].T
-    v_copy.wait()
-    vt[1 - head] = v_all[theirs, :].T
-
-    def forward(p, carry):
-        cols = pl.ds(pl.multiple_of(p * LANES, LANES), LANES)
-        left = jnp.concatenate([k_all[:, cols], mask_k[...]], axis=1)
+
+    far = 1 - head
+    blocks = share // LANES
+    half = LANES // 2
+
+    def raw_scores(p, side, shift):
+        left = jnp.concatenate(
+            [k_all[side, :, p * LANES : (p + 1) * LANES], mask_k[side]], axis=1
+        )
         right = jnp.concatenate(
             [qs[p], jnp.concatenate([mask_q[...], mask_q[...]], axis=0)], axis=1
         )
         raw = dot(left, right, NT)
         bands = []
-        for kb in range(slot // LANES):
-            blocks = []
+        for kb in range(blocks):
+            parts_of = []
             for a in range(2):
-                for qb in range(share // LANES):
-                    apart = kb - (head * (share // LANES) + qb)
-                    spot = jnp.clip(apart, -2, 2) + 2
+                for qb in range(blocks):
+                    apart = shift + (kb - qb)
+                    if isinstance(apart, int):
+                        spot = min(max(apart, -2), 2) + 2
+                    else:
+                        spot = jnp.clip(apart, -2, 2) + 2
                     lo = a * share + qb * LANES
-                    blocks.append(
+                    parts_of.append(
                         raw[kb * LANES : (kb + 1) * LANES, lo : lo + LANES] + bias[2 * p + a, spot]
                     )
-            bands.append(jnp.concatenate(blocks, axis=1))
-        scores = jnp.concatenate(bands, axis=0)
-        expo = jnp.exp(scores - jnp.max(scores, axis=0, keepdims=True))
-        prob = expo * (1.0 / jnp.sum(expo, axis=0, keepdims=True))
-        probs[p] = prob
-        low = prob.astype(bf16)
-        half = LANES // 2
+            bands.append(jnp.concatenate(parts_of, axis=1))
+        return jnp.concatenate(bands, axis=0)
+
+    for p in range(pairs):
+        probs[p, head] = raw_scores(p, head, 0)
+    kt[head] = k_all[head].T
+    vt[head] = v_all[head].T
+    k_copy.wait()
+    kt[far] = k_all[far].T
+    v_copy.wait()
+    vt[far] = v_all[far].T
+
+    for p in range(pairs):
+        near_raw = probs[p, head]
+        far_raw = raw_scores(p, far, (1 - 2 * head) * blocks)
+        top = jnp.maximum(
+            jnp.max(near_raw, axis=0, keepdims=True), jnp.max(far_raw, axis=0, keepdims=True)
+        )
+        near_exp, far_exp = jnp.exp(near_raw - top), jnp.exp(far_raw - top)
+        inverse = 1.0 / (
+            jnp.sum(near_exp, axis=0, keepdims=True) + jnp.sum(far_exp, axis=0, keepdims=True)
+        )
+        near_prob, far_prob = near_exp * inverse, far_exp * inverse
+        probs[p, head] = near_prob
+        probs[p, far] = far_prob
+        near_low, far_low = near_prob.astype(bf16), far_prob.astype(bf16)
         for a in range(2):
-            side = low[:, a * share : (a + 1) * share]
-            feat = pl.ds(pl.multiple_of(p * LANES + a * half, half), half)
+            feat = slice(p * LANES + a * half, p * LANES + (a + 1) * half)
+            side = slice(a * share, (a + 1) * share)
             att_t[feat, :] = (
-                dot(vt[0, feat, :], side[:share]) + dot(vt[1, feat, :], side[share:])
+                dot(vt[head, feat, :], near_low[:, side]) + dot(vt[far, feat, :], far_low[:, side])
             ).astype(bf16)
-        return carry
-
-    lax.fori_loop(0, pairs, forward, 0, unroll=True)
+
     far_copies[2].wait()
     x1 = x0[...] + dot(att_t[...].T, wout[...])
     n2 = rms_scale(x1, ff_gain).astype(bf16)
@@ -412,60 +442,66 @@
         dxb[p, :share, :] = jnp.where(lane < LANES // 2, part, jnp.zeros_like(part))
         dxb[p, share:, :] = jnp.where(lane >= LANES // 2, part, jnp.zeros_like(part))
 
-    def send_of(p):
+    def first_sends(p):
         return [
-            remote(src.at[p], dst.at[p], dkv_send.at[i, p], dkv_recv.at[i, p], other)
+            remote(src.at[0, p], dst.at[0, p], dkv_send.at[i, p], dkv_recv.at[i, p], other)
             for i, (src, dst) in enumerate(((dk_send, dk_recv), (dv_send, dv_recv)))
         ]
 
-    def query_grad(p, d_score, begin, end):
-        half = LANES // 2
+    last_sends = [
+        remote(src.at[1], dst.at[1], dkv_send.at[i, pairs], dkv_recv.at[i, pairs], other)
+        for i, (src, dst) in enumerate(((dk_send, dk_recv), (dv_send, dv_recv)))
+    ]
+    first_rows, last_rows = slice(0, LANES), slice(LANES, share)
+
+    def query_grad(p, begin, end):
         for a in range(2):
-            side = d_score[:, a * share + begin : a * share + end]
-            feat = pl.ds(pl.multiple_of(p * LANES + a * half, half), half)
+            feat = slice(p * LANES + a * half, p * LANES + (a + 1) * half)
+            side = slice(a * share + begin, a * share + end)
             att_t[feat, begin:end] = (
-                (dot(kt[0, feat, :], side[:share]) + dot(kt[1, feat, :], side[share:])) * 0.125
+                (
+                    dot(kt[head, feat, :], d_scores[p, head, :, side])
+                    + dot(kt[far, feat, :], d_scores[p, far, :, side])
+                )
+                * 0.125
             ).astype(bf16)
 
-    def backward(p, carry):
-        cols = pl.ds(pl.multiple_of(p * LANES, LANES), LANES)
+    for p in range(pairs):
+        cols = slice(p * LANES, (p + 1) * LANES)
         d_out = dxb[p]
-        d_prob = dot(v_all[:, cols], d_out, NT)
-        prob = probs[p]
-        delta = jnp.sum(prob * d_prob, axis=0, keepdims=True)
-        d_score = (prob * (d_prob - delta)).astype(bf16)
-        low = prob.astype(bf16)
-        d_scores[p] = d_score
-        query_grad(p, d_score, 0, LANES)
-        d_v = dot(low, d_out)
-        d_k = dot(d_score, qs[p])
-        first = head == 0
-        dv_own[p] = jnp.where(first, d_v[:share], d_v[share:])
-        dk_own[p] = jnp.where(first, d_k[:share], d_k[share:])
-        dv_send[p] = jnp.where(first, d_v[share:], d_v[:share])
-        dk_send[p] = jnp.where(first, d_k[share:], d_k[:share])
-        for copy in send_of(p):
+        near_d = dot(v_all[head, :, cols], d_out, NT)
+        far_d = dot(v_all[far, :, cols], d_out, NT)
+        near_prob, far_prob = probs[p, head], probs[p, far]
+        delta = jnp.sum(near_prob * near_d, axis=0, keepdims=True) + jnp.sum(
+            far_prob * far_d, axis=0, keepdims=True
+        )
+        far_score = (far_prob * (far_d - delta)).astype(bf16)
+        d_scores[p, far] = far_score
+        d_scores[p, head] = (near_prob * (near_d - delta)).astype(bf16)
+        dv_send[0, p] = dot(far_prob[first_rows].astype(bf16), d_out)
+        dk_send[0, p] = dot(far_score[first_rows], qs[p])
+        for copy in first_sends(p):
             copy.start()
-        return carry
-
-    lax.fori_loop(0, pairs, backward, 0, unroll=True)
-
-    def input_grad(part):
+    for p in range(pairs):
+        dv_own[0, p] = dot(probs[p, head, first_rows].astype(bf16), dxb[p])
+        dk_own[0, p] = dot(d_scores[p, head, first_rows], qs[p])
+        query_grad(p, 0, LANES)
+
+    def input_grad(index, part):
         d_k = jnp.concatenate(
-            [(dk_own[p, part] + dk_recv[p, part]).astype(bf16) for p in range(pairs)], axis=1
+            [(dk_own[index, p] + dk_recv[index, p]).astype(bf16) for p in range(pairs)], axis=1
         )
         d_v = jnp.concatenate(
-            [(dv_own[p, part] + dv_recv[p, part]).astype(bf16) for p in range(pairs)], axis=1
+            [(dv_own[index, p] + dv_recv[index, p]).astype(bf16) for p in range(pairs)], axis=1
         )
         d_n1 = acc_dn[part] + dot(d_k, wqkv[1], NT) + dot(d_v, wqkv[2], NT)
         grad_buf[part] = grad_buf[part] + rms_back(x0[part], attn_gain, d_n1)
 
-    first_rows, last_rows = slice(0, LANES), slice(LANES, share)
     acc_dn[first_rows] = dot(att_t[:, first_rows].T, wqkv[0], NT)
     for p in range(pairs):
-        for copy in send_of(p):
+        for copy in first_sends(p):
             copy.wait()
-    input_grad(first_rows)
+    input_grad(0, first_rows)
 
     chunks, chunk_rows, chunk_cols = total.shape
 
@@ -485,12 +521,18 @@
         target = lax.rem(my_out + k, outer)
         return target, (target * inner + my_in, head)
 
-    mine_in = jnp.minimum(my_in, chunks - 1)
+    skip = (inner - chunks) // 2
+
+    def chunk_of(place):
+        index = place - skip
+        return jnp.clip(index, 0, chunks - 1), (index >= 0) & (index < chunks)
+
+    mine_in, sums = chunk_of(my_in)
 
     def scatter_to(k):
         target, device = in_peer(k)
-        at = jnp.minimum(target, chunks - 1)
-        return target, remote(rs_send.at[at], parts.at[my_in], send1.at[k], recv1.at[my_in], device)
+        at, holds = chunk_of(target)
+        return holds, remote(rs_send.at[at], parts.at[my_in], send1.at[k], recv1.at[my_in], device)
 
     def scatter_from(k):
         source, device = in_peer(k)
@@ -503,8 +545,8 @@
 
     def gather_from(k):
         source, device = in_peer(k)
-        at = jnp.minimum(source, chunks - 1)
-        return source, at, remote(total.at[at], total.at[at], send2.at[k], recv2.at[at], device)
+        at, holds = chunk_of(source)
+        return holds, at, remote(total.at[at], total.at[at], send2.at[k], recv2.at[at], device)
 
     def across(k):
         return remote(
@@ -520,27 +562,34 @@
 
     @pl.when(head == 0)
     def _():
-        local = dot(order, grad_buf[first_rows], TN, exact_mode).astype(bf16)
+        rounded = grad_buf[first_rows].astype(bf16)
+        local = dot(order.astype(bf16), rounded, TN).astype(bf16)
         for c in range(chunks):
-            top, left = (c // 2) * chunk_rows, (c % 2) * chunk_cols
-            rs_send[c] = local[top : top + chunk_rows, left : left + chunk_cols]
+            rs_send[c] = local[c * chunk_rows : (c + 1) * chunk_rows]
 
         for k in range(1, inner):
-            target, copy = scatter_to(k)
-
-            @pl.when(target < chunks)
+            holds, copy = scatter_to(k)
+
+            @pl.when(holds)
             def _():
                 copy.start()
 
     for p in range(pairs):
-        query_grad(p, d_scores[p], LANES, share)
+        dv_send[1, p] = dot(probs[p, far, last_rows].astype(bf16), dxb[p])
+        dk_send[1, p] = dot(d_scores[p, far, last_rows], qs[p])
+    for copy in last_sends:
+        copy.start()
+    for p in range(pairs):
+        dv_own[1, p] = dot(probs[p, head, last_rows].astype(bf16), dxb[p])
+        dk_own[1, p] = dot(d_scores[p, head, last_rows], qs[p])
+        query_grad(p, LANES, share)
     for i in range(ff // ff_block):
         out_buf[...] = out_buf[...] + dot(act[i], wdown[i * ff_block : (i + 1) * ff_block, :])
     out_low[...] = out_buf[...].astype(bf16)
     out_copy = pltpu.make_async_copy(out_low, out_hbm, out_sem.at[0])
     out_copy.start()
 
-    @pl.when((head == 0) & (my_in < chunks))
+    @pl.when((head == 0) & sums)
     def _():
         parts[my_in] = rs_send[mine_in]
         for k in range(1, inner):
@@ -565,16 +614,18 @@
         forward_of(mine_in).start()
 
     acc_dn[last_rows] = dot(att_t[:, last_rows].T, wqkv[0], NT)
-    input_grad(last_rows)
+    for copy in last_sends:
+        copy.wait()
+    input_grad(1, last_rows)
     grad_copy = pltpu.make_async_copy(grad_buf, grad_hbm, out_sem.at[1])
     grad_copy.start()
 
     @pl.when(head == 0)
     def _():
         for k in range(1, inner):
-            source, at, copy = gather_from(k)
-
-            @pl.when(source < chunks)
+            holds, at, copy = gather_from(k)
+
+            @pl.when(holds)
             def _():
                 copy.wait_recv()
                 forward_of(at).start()
@@ -593,13 +644,13 @@
     @pl.when(head == 0)
     def _():
         for k in range(1, inner):
-            target, device = in_peer(k)
-
-            @pl.when(target < chunks)
+            holds, copy = scatter_to(k)
+
+            @pl.when(holds)
             def _():
-                scatter_to(k)[1].wait_send()
-
-        @pl.when(my_in < chunks)
+                copy.wait_send()
+
+        @pl.when(sums)
         def _():
             for k in range(1, inner):
                 gather_to(k).wait_send()
@@ -617,7 +668,7 @@
 
 
 def run_layer(
-    groups, ids, segments, ag, fg, rel, valid, prompt, cot, table, wqkv, wout, win, wdown
+    groups, valid, ids, segments, ag, fg, rel, prompt, cot, table, wqkv, wout, win, wdown
 ):
     share, width = cot.shape
     ff = 2 * win.shape[1]
@@ -629,8 +680,8 @@
     block = -(-capacity // 16) * 16
     inner = math.gcd(groups, 16)
     outer = groups // inner
-    chunk_rows, chunk_cols = 16, width // 2
-    chunks = 2 * -(-rows // chunk_rows)
+    chunk_rows, chunk_cols = 16, width
+    chunks = -(-rows // chunk_rows)
     in_vmem = pl.BlockSpec(memory_space=pltpu.VMEM)
     in_hbm = pl.BlockSpec(memory_space=pl.ANY)
     dma = pltpu.SemaphoreType.DMA
@@ -641,9 +692,14 @@
             jax.ShapeDtypeStruct((share, width), f32),
             jax.ShapeDtypeStruct((chunks, chunk_rows, chunk_cols), bf16),
         ),
-        in_specs=[in_vmem] * 5 + [pl.BlockSpec(memory_space=pltpu.SMEM)] + [in_hbm] * 7,
+        in_specs=[pl.BlockSpec(memory_space=pltpu.SMEM)] + [in_hbm] * 12,
         out_specs=[in_hbm] * 3,
         scratch_shapes=[
+            vmem(*ids.shape, dtype=jnp.int32),
+            vmem(*segments.shape, dtype=jnp.int32),
+            vmem(*ag.shape),
+            vmem(*fg.shape),
+            vmem(*rel.shape, dtype=bf16),
             vmem(*table.shape, dtype=bf16),
             vmem(3, width, width, dtype=bf16),
             vmem(width, width, dtype=bf16),
@@ -659,34 +715,34 @@
             vmem(share, width, dtype=bf16),
             vmem(1, slot, dtype=jnp.int32),
             vmem(1, slot),
-            vmem(slot, LANES, dtype=bf16),
+            vmem(2, share, LANES, dtype=bf16),
             vmem(share, LANES, dtype=bf16),
             vmem(share, width),
             vmem(LANES, width),
             vmem(ff // ff_block, share, ff_block),
             vmem(ff // ff_block, share, ff_block, dtype=bf16),
-            vmem(pairs, slot, slot, dtype=bf16),
+            vmem(pairs, 2, share, slot, dtype=bf16),
             vmem(share, width),
             vmem(share, width),
-            vmem(slot, width, dtype=bf16),
-            vmem(slot, width, dtype=bf16),
+            vmem(2, share, width, dtype=bf16),
+            vmem(2, share, width, dtype=bf16),
             vmem(2, width, share, dtype=bf16),
             vmem(2, width, share, dtype=bf16),
             vmem(pairs, slot, LANES, dtype=bf16),
             vmem(2 * pairs, 5, LANES, LANES),
-            vmem(pairs, slot, slot),
+            vmem(pairs, 2, share, slot),
             vmem(width, share, dtype=bf16),
             vmem(share, width),
             vmem(share, width, dtype=bf16),
         ]
-        + [vmem(pairs, share, LANES)] * 6
+        + [vmem(2, pairs, LANES, LANES)] * 6
         + [
             vmem(pairs, slot, LANES, dtype=bf16),
             vmem(chunks, chunk_rows, chunk_cols, dtype=bf16),
             vmem(inner, chunk_rows, chunk_cols, dtype=bf16),
             vmem(outer, chunk_rows, chunk_cols),
             vmem(chunks, chunk_rows, chunk_cols, dtype=bf16),
-            dma((7,)),
+            dma((12,)),
             dma((5,)),
             dma((5,)),
             dma((groups,)),
@@ -695,8 +751,8 @@
             dma((groups,)),
             dma((2,)),
             dma((2,)),
-            dma((2, pairs)),
-            dma((2, pairs)),
+            dma((2, pairs + 1)),
+            dma((2, pairs + 1)),
             dma((inner,)),
             dma((inner,)),
             dma((inner,)),
@@ -711,7 +767,7 @@
             collective_id=1, has_side_effects=True, vmem_limit_bytes=60 * 2**20
         ),
         name="layer",
-    )(ids, segments, ag, fg, rel, valid, prompt, cot, table, wqkv, wout, win, wdown)
+    )(valid, ids, segments, ag, fg, rel, prompt, cot, table, wqkv, wout, win, wdown)
 
 
 def finish_kernel(
@@ -739,15 +795,8 @@
         stores[-1].start()
 
     rows = prompt_ref.shape[0]
-    chunks = total_ref.shape[0]
     loads[0].wait()
-    summed = jnp.concatenate(
-        [
-            jnp.concatenate([total_ref[c], total_ref[c + 1]], axis=1)
-            for c in range(0, chunks, 2)
-        ],
-        axis=0,
-    ).astype(f32)[:rows]
+    summed = total_ref[...].reshape(-1, total_ref.shape[2]).astype(f32)[:rows]
     grad_ref[...] = summed
     store(grad_ref, 2)
     norm = jnp.sqrt(jnp.sum(summed * summed, keepdims=True))
@@ -840,7 +889,7 @@
     groups = lax.axis_size("dp")
     rows, width = prompt.shape
     out, grad, total = run_layer(
-        groups, ids, segments, attn_gain, ff_gain, rel_bias.T, valid_rows, prompt, cotangent, table,
+        groups, valid_rows, ids, segments, attn_gain, ff_gain, rel_bias.T, prompt, cotangent, table,
         jnp.transpose(w_qkv, (1, 0, 2)), w_out, w_in, w_down,
     )
     clip_at = clip_share * math.sqrt(rows * width * groups)

time: 68.5 us -> 66.3 us (0.968)
  Pallas kernels: 66.8 us -> 64.7 us
    pallas_call x1, Pallas kernels: 64 us -> 61.9 us  [run_layer(): pl.pallas_call(functools.partial(layer_kernel, groups, inner, block, rows...]
where the time goes in v4:
time: 66.3 us; the launch traced here: 66.2 us
  Pallas kernels  64.7 us (98%)
  between operations  1.45 us (2%)
    pallas_call x1, Pallas kernels, run_layer(): pl.pallas_call(functools.partial(layer_kernel, groups, inner, block, rows...  61.9 us
    pallas_call x1, Pallas kernels, run_finish(): pl.pallas_call(functools.partial(finish_kernel, clip_at), out_shape=(jax....  2.79 us

profile of v4, /device:TPU:1, one launch (start us, length us, event | category | flops | bytes accessed | tf_op | source)
XLA Modules:
  0.0 66.2 jit_solution(10321351983571352464)
XLA Ops:
  1.3 61.9 %layer.1 = (bf16[256,768]{1,0:T(8,128)(2,1)}, f32[256,768]{1,0:T(8,128)}, bf16[7,16,768]{2,1,0:T(8,128)(2,1)}) custom-call(s32[1]{0:T(128)S(6)} %copy.23.valid_ref, s32[1,512]{1,0:T(1,128)} %ids_hbm.1, s32[1,412]{1,0:T(1,128)} %seg_hbm.1, f32[768]{0:T(1024)} %ag_hbm.1, f32[768]{0:T(1024)} %fg_hbm.1, bf16[6,32]{1,0:T(8,128)(2,1)} %bitcast.4, ...), custom_call_target="tpu_custom_call" | custom-call | tf_op jit(solution)/shard_map/layer/pallas_call | solution.py:688
  63.2 2.8 %finish.1 = (bf16[256,768]{1,0:T(8,128)(2,1)}, f32[256,768]{1,0:T(8,128)}, f32[100,768]{1,0:T(8,128)}, f32[1,1]{1,0:T(1,128)}, f32[100,768]{1,0:T(8,128)}, /*ind...) custom-call(f32[100,768]{1,0:T(8,128)} %prompt_hbm.3, f32[100,768]{1,0:T(8,128)} %first_hbm.1, ...), custom_call_target="tpu_custom_call" | custom-call | tf_op jit(solution)/shard_map/finish/pallas_call | solution.py:837

commit v5 on v4

--- a/solution.py
+++ b/solution.py
@@ -392,9 +392,11 @@
     v_copy.wait()
     vt[far] = v_all[far].T
 
+    far_next = raw_scores(0, far, (1 - 2 * head) * blocks)
     for p in range(pairs):
-        near_raw = probs[p, head]
-        far_raw = raw_scores(p, far, (1 - 2 * head) * blocks)
+        near_raw, far_raw = probs[p, head], far_next
+        if p + 1 < pairs:
+            far_next = raw_scores(p + 1, far, (1 - 2 * head) * blocks)
         top = jnp.maximum(
             jnp.max(near_raw, axis=0, keepdims=True), jnp.max(far_raw, axis=0, keepdims=True)
         )
@@ -418,23 +420,25 @@
     n2 = rms_scale(x1, ff_gain).astype(bf16)
     far_copies[3].wait()
     out_buf[...] = x1
-    acc_dn[...] = jnp.zeros_like(acc_dn)
-
-    def feed(i, carry):
-        at = pl.ds(pl.multiple_of(i * ff_block, ff_block), ff_block)
-        u = dot(n2, win[:, at])
+    d_n2 = None
+    ff_blocks = ff // ff_block
+    units = [slice(i * ff_block, (i + 1) * ff_block) for i in range(ff_blocks)]
+    u_next = dot(n2, win[:, units[0]])
+    for i in range(ff_blocks):
+        u = u_next
+        if i + 1 < ff_blocks:
+            u_next = dot(n2, win[:, units[i + 1]])
         square = u * u
-        t = jnp.tanh(GELU_C * (u + 0.044715 * (u * square)))
-        act[i] = (0.5 * u * (1.0 + t)).astype(bf16)
-        slope = 0.5 * (1.0 + t) + 0.5 * u * (1.0 - t * t) * (
-            GELU_C * (1.0 + 3 * 0.044715 * square)
+        t = jnp.tanh(u * (GELU_C + (GELU_C * 0.044715) * square))
+        half_u = 0.5 * u
+        act[i] = (half_u + half_u * t).astype(bf16)
+        slope = (0.5 + 0.5 * t) + (half_u * (1.0 - t * t)) * (
+            GELU_C + (GELU_C * 3 * 0.044715) * square
         )
         d_hidden = (d_act[i] * slope).astype(bf16)
-        acc_dn[...] += dot(d_hidden, win[:, at], NT)
-        return carry
-
-    lax.fori_loop(0, ff // ff_block, feed, 0, unroll=True)
-    dx1 = dy.astype(f32) + rms_back(x1, ff_gain, acc_dn[...])
+        piece = dot(d_hidden, win[:, units[i]], NT)
+        d_n2 = piece if d_n2 is None else d_n2 + piece
+    dx1 = dy.astype(f32) + rms_back(x1, ff_gain, d_n2)
     grad_buf[...] = dx1
     d_att = dot(dx1.astype(bf16), wout[...], NT).astype(bf16)
     for p in range(pairs):
@@ -466,11 +470,16 @@
                 * 0.125
             ).astype(bf16)
 
+    def prob_grads(p):
+        cols = slice(p * LANES, (p + 1) * LANES)
+        return [dot(v_all[side, :, cols], dxb[p], NT) for side in (head, far)]
+
+    d_next = prob_grads(0)
     for p in range(pairs):
-        cols = slice(p * LANES, (p + 1) * LANES)
         d_out = dxb[p]
-        near_d = dot(v_all[head, :, cols], d_out, NT)
-        far_d = dot(v_all[far, :, cols], d_out, NT)
+        near_d, far_d = d_next
+        if p + 1 < pairs:
+            d_next = prob_grads(p + 1)
         near_prob, far_prob = probs[p, head], probs[p, far]
         delta = jnp.sum(near_prob * near_d, axis=0, keepdims=True) + jnp.sum(
             far_prob * far_d, axis=0, keepdims=True

time: 66.3 us -> 64.9 us (0.979)
  Pallas kernels: 64.7 us -> 63.3 us
    pallas_call x1, Pallas kernels: 61.9 us -> 60.5 us  [run_layer(): pl.pallas_call(functools.partial(layer_kernel, groups, inner, block, rows...]
where the time goes in v5:
time: 64.9 us; the launch traced here: 64.8 us
  Pallas kernels  63.3 us (98%)
  between operations  1.45 us (2%)
    pallas_call x1, Pallas kernels, run_layer(): pl.pallas_call(functools.partial(layer_kernel, groups, inner, block, rows...  60.5 us
    pallas_call x1, Pallas kernels, run_finish(): pl.pallas_call(functools.partial(finish_kernel, clip_at), out_shape=(jax....  2.79 us

profile of v5, /device:TPU:1, one launch (start us, length us, event | category | flops | bytes accessed | tf_op | source)
XLA Modules:
  0.0 64.8 jit_solution(15001151197531479616)
XLA Ops:
  1.3 60.5 %layer.1 = (bf16[256,768]{1,0:T(8,128)(2,1)}, f32[256,768]{1,0:T(8,128)}, bf16[7,16,768]{2,1,0:T(8,128)(2,1)}) custom-call(s32[1]{0:T(128)S(6)} %copy.23.valid_ref, s32[1,512]{1,0:T(1,128)} %ids_hbm.1, s32[1,412]{1,0:T(1,128)} %seg_hbm.1, f32[768]{0:T(1024)} %ag_hbm.1, f32[768]{0:T(1024)} %fg_hbm.1, bf16[6,32]{1,0:T(8,128)(2,1)} %bitcast.4, ...), custom_call_target="tpu_custom_call" | custom-call | tf_op jit(solution)/shard_map/layer/pallas_call | solution.py:697
  61.8 2.8 %finish.1 = (bf16[256,768]{1,0:T(8,128)(2,1)}, f32[256,768]{1,0:T(8,128)}, f32[100,768]{1,0:T(8,128)}, f32[1,1]{1,0:T(1,128)}, f32[100,768]{1,0:T(8,128)}, /*ind...) custom-call(f32[100,768]{1,0:T(8,128)} %prompt_hbm.3, f32[100,768]{1,0:T(8,128)} %first_hbm.1, ...), custom_call_target="tpu_custom_call" | custom-call | tf_op jit(solution)/shard_map/finish/pallas_call | solution.py:846

commit v6 on v5

--- a/solution.py
+++ b/solution.py
@@ -66,7 +66,7 @@
     req_out, req_in, found, fetched, rel_all, prompt_in, prompt_pad, cot, seg_pad, seg_here, mask_k, mask_q,
     x0, x0_prompt, d_act, act, d_scores, out_buf, grad_buf,
     k_all, v_all, kt, vt, qs, bias, probs, att_t, acc_dn, out_low,
-    dk_own, dv_own, dk_send, dv_send, dk_recv, dv_recv, dxb,
+    dk_own, dv_own, d_send, d_recv, dxb,
     rs_send, parts, across_buf, total,
     load_sem, far_send, far_recv, req_send, req_recv, row_send, row_recv,
     kv_send, kv_recv, dkv_send, dkv_recv,
@@ -446,16 +446,12 @@
         dxb[p, :share, :] = jnp.where(lane < LANES // 2, part, jnp.zeros_like(part))
         dxb[p, share:, :] = jnp.where(lane >= LANES // 2, part, jnp.zeros_like(part))
 
-    def first_sends(p):
-        return [
-            remote(src.at[0, p], dst.at[0, p], dkv_send.at[i, p], dkv_recv.at[i, p], other)
-            for i, (src, dst) in enumerate(((dk_send, dk_recv), (dv_send, dv_recv)))
-        ]
-
-    last_sends = [
-        remote(src.at[1], dst.at[1], dkv_send.at[i, pairs], dkv_recv.at[i, pairs], other)
-        for i, (src, dst) in enumerate(((dk_send, dk_recv), (dv_send, dv_recv)))
-    ]
+    def first_send(p):
+        return remote(d_send.at[0, p], d_recv.at[0, p], dkv_send.at[p], dkv_recv.at[p], other)
+
+    last_send = remote(
+        d_send.at[1], d_recv.at[1], dkv_send.at[pairs], dkv_recv.at[pairs], other
+    )
     first_rows, last_rows = slice(0, LANES), slice(LANES, share)
 
     def query_grad(p, begin, end):
@@ -487,10 +483,9 @@
         far_score = (far_prob * (far_d - delta)).astype(bf16)
         d_scores[p, far] = far_score
         d_scores[p, head] = (near_prob * (near_d - delta)).astype(bf16)
-        dv_send[0, p] = dot(far_prob[first_rows].astype(bf16), d_out)
-        dk_send[0, p] = dot(far_score[first_rows], qs[p])
-        for copy in first_sends(p):
-            copy.start()
+        d_send[0, p, 1] = dot(far_prob[first_rows].astype(bf16), d_out)
+        d_send[0, p, 0] = dot(far_score[first_rows], qs[p])
+        first_send(p).start()
     for p in range(pairs):
         dv_own[0, p] = dot(probs[p, head, first_rows].astype(bf16), dxb[p])
         dk_own[0, p] = dot(d_scores[p, head, first_rows], qs[p])
@@ -498,18 +493,17 @@
 
     def input_grad(index, part):
         d_k = jnp.concatenate(
-            [(dk_own[index, p] + dk_recv[index, p]).astype(bf16) for p in range(pairs)], axis=1
+            [(dk_own[index, p] + d_recv[index, p, 0]).astype(bf16) for p in range(pairs)], axis=1
         )
         d_v = jnp.concatenate(
-            [(dv_own[index, p] + dv_recv[index, p]).astype(bf16) for p in range(pairs)], axis=1
+            [(dv_own[index, p] + d_recv[index, p, 1]).astype(bf16) for p in range(pairs)], axis=1
         )
         d_n1 = acc_dn[part] + dot(d_k, wqkv[1], NT) + dot(d_v, wqkv[2], NT)
         grad_buf[part] = grad_buf[part] + rms_back(x0[part], attn_gain, d_n1)
 
     acc_dn[first_rows] = dot(att_t[:, first_rows].T, wqkv[0], NT)
     for p in range(pairs):
-        for copy in first_sends(p):
-            copy.wait()
+        first_send(p).wait()
     input_grad(0, first_rows)
 
     chunks, chunk_rows, chunk_cols = total.shape
@@ -584,10 +578,9 @@
                 copy.start()
 
     for p in range(pairs):
-        dv_send[1, p] = dot(probs[p, far, last_rows].astype(bf16), dxb[p])
-        dk_send[1, p] = dot(d_scores[p, far, last_rows], qs[p])
-    for copy in last_sends:
-        copy.start()
+        d_send[1, p, 1] = dot(probs[p, far, last_rows].astype(bf16), dxb[p])
+        d_send[1, p, 0] = dot(d_scores[p, far, last_rows], qs[p])
+    last_send.start()
     for p in range(pairs):
         dv_own[1, p] = dot(probs[p, head, last_rows].astype(bf16), dxb[p])
         dk_own[1, p] = dot(d_scores[p, head, last_rows], qs[p])
@@ -623,8 +616,7 @@
         forward_of(mine_in).start()
 
     acc_dn[last_rows] = dot(att_t[:, last_rows].T, wqkv[0], NT)
-    for copy in last_sends:
-        copy.wait()
+    last_send.wait()
     input_grad(1, last_rows)
     grad_copy = pltpu.make_async_copy(grad_buf, grad_hbm, out_sem.at[1])
     grad_copy.start()
@@ -744,7 +736,8 @@
             vmem(share, width),
             vmem(share, width, dtype=bf16),
         ]
-        + [vmem(2, pairs, LANES, LANES)] * 6
+        + [vmem(2, pairs, LANES, LANES)] * 2
+        + [vmem(2, pairs, 2, LANES, LANES)] * 2
         + [
             vmem(pairs, slot, LANES, dtype=bf16),
             vmem(chunks, chunk_rows, chunk_cols, dtype=bf16),
@@ -760,8 +753,8 @@
             dma((groups,)),
             dma((2,)),
             dma((2,)),
-            dma((2, pairs + 1)),
-            dma((2, pairs + 1)),
+            dma((pairs + 1,)),
+            dma((pairs + 1,)),
             dma((inner,)),
             dma((inner,)),
             dma((inner,)),

time: 64.9 us -> 64.8 us (level)
  no operation moved by 1% of the time
where the time goes in v6:
time: 64.8 us; the launch traced here: 64.6 us
  Pallas kernels  63.2 us (98%)
  between operations  1.45 us (2%)
    pallas_call x1, Pallas kernels, run_layer(): pl.pallas_call(functools.partial(layer_kernel, groups, inner, block, rows...  60.4 us
    pallas_call x1, Pallas kernels, run_finish(): pl.pallas_call(functools.partial(finish_kernel, clip_at), out_shape=(jax....  2.79 us

profile of v6, /device:TPU:1, one launch (start us, length us, event | category | flops | bytes accessed | tf_op | source)
XLA Modules:
  0.0 64.6 jit_solution(3082559353025173730)
XLA Ops:
  1.3 60.4 %layer.1 = (bf16[256,768]{1,0:T(8,128)(2,1)}, f32[256,768]{1,0:T(8,128)}, bf16[7,16,768]{2,1,0:T(8,128)(2,1)}) custom-call(s32[1]{0:T(128)S(6)} %copy.23.valid_ref, s32[1,512]{1,0:T(1,128)} %ids_hbm.1, s32[1,412]{1,0:T(1,128)} %seg_hbm.1, f32[768]{0:T(1024)} %ag_hbm.1, f32[768]{0:T(1024)} %fg_hbm.1, bf16[6,32]{1,0:T(8,128)(2,1)} %bitcast.4, ...), custom_call_target="tpu_custom_call" | custom-call | tf_op jit(solution)/shard_map/layer/pallas_call | solution.py:689
  61.7 2.8 %finish.1 = (bf16[256,768]{1,0:T(8,128)(2,1)}, f32[256,768]{1,0:T(8,128)}, f32[100,768]{1,0:T(8,128)}, f32[1,1]{1,0:T(1,128)}, f32[100,768]{1,0:T(8,128)}, /*ind...) custom-call(f32[100,768]{1,0:T(8,128)} %prompt_hbm.3, f32[100,768]{1,0:T(8,128)} %first_hbm.1, ...), custom_call_target="tpu_custom_call" | custom-call | tf_op jit(solution)/shard_map/finish/pallas_call | solution.py:839
